TPU v7x, 512 devices: a whole 4x4x16 slice. The times are simulated.
512 devices in a mesh: wide: 64 (over z, x), hot: 8 (over y, core).
Axes of the slice: x: 4, y: 4, z: 16, core: 2. Of those that a mesh axis runs over, the one named last changes fastest.
Arguments:
- paper_features: bfloat16 [524288, 768], P(('wide', 'hot')), may hold values from -24 to 24
- self_weight: bfloat16 [768, 256], replicated, may hold values from -0.21875 to 0.21875
- cite_weight: bfloat16 [768, 256], replicated, may hold values from -0.21875 to 0.21875
- hot_embed: float32 [1024, 256], P('hot'), may hold values from -6 to 6
- hot_ids: int32 [524288, 8], P(('wide', 'hot')), may hold values from 0 to 1023
- tile_values: bfloat16 [16384, 128, 128], P(('wide', 'hot')), may hold values from 0 to 1, as said below
- tile_rows: int32 [16384], P(('wide', 'hot')), may hold values from 0 to 128
- tile_target_block: int32 [16384], P(('wide', 'hot')), may hold values from 0 to 7
- tile_block: int32 [16384], P(('wide', 'hot')), may hold values from 0 to 7
- tile_owner: int32 [16384], P(('wide', 'hot')), may hold values from 0 to 63, as said below
- cotangent: bfloat16 [524288, 256], P(('wide', 'hot')), may hold values from -6 to 6
Outputs:
- hidden: bfloat16 [524288, 256], P(('wide', 'hot'))
- self_grad: float32 [768, 256], P('wide')
- cite_grad: float32 [768, 256], P('wide')
- author_grad: float32 [1024, 256], P('hot')
Inputs may be any that keep to these rules, and one draw needn't show every extreme that they name: Within each device's 32 tiles no value of tile_owner appears more than 1 times, and one value appears exactly 1 times. Tile rows at or past tile_rows are padding. `tile_values`: edge weights lie in [0, 1]; most entries are zero.
All inputs are finite; a program needn't handle non-finite values.
Results may differ from a plain program's by a relative error of at most 0.0059.
Values may be sent and summed in bfloat16 or wider, within the bound.
A program may use at most 128 MiB of HBM per device.

v0:
```python
import jax
import jax.numpy as jnp
from jax import lax
from jax.sharding import PartitionSpec as P

HK = 8


def on_device(
    paper_features,
    self_weight,
    cite_weight,
    hot_embed,
    hot_ids,
    tile_values,
    tile_rows,
    tile_target_block,
    tile_block,
    tile_owner,
    cotangent,
):
    wide_size = lax.axis_size("wide")
    tile_total = tile_values.shape[0]
    tile_size = tile_values.shape[1]
    row_total, feat_in = paper_features.shape
    feat_out = self_weight.shape[1]
    block_total = row_total // tile_size
    slot_cap = 2 * tile_total // wide_size
    slot_total = wide_size * slot_cap
    owner_hot = (tile_owner[:, None] == jnp.arange(wide_size, dtype=jnp.int32)[None, :]).astype(
        jnp.int32
    )
    earlier = jnp.cumsum(owner_hot, axis=0) - owner_hot
    slot_rank = jnp.sum(earlier * owner_hot, axis=1)
    slot_index = tile_owner * slot_cap + slot_rank
    placement = slot_index[:, None] == jnp.arange(slot_total, dtype=jnp.int32)[None, :]
    wanted = jnp.sum(placement.astype(jnp.int32) * tile_block[:, None], axis=0)
    asked_blocks = lax.all_to_all(
        wanted.reshape(wide_size, slot_cap), "wide", split_axis=0, concat_axis=0, tiled=True
    ).reshape(slot_total)
    live_rows = jnp.arange(tile_size, dtype=jnp.int32)[None, :, None] < tile_rows[:, None, None]
    masked_values = jnp.where(live_rows, tile_values, jnp.zeros((), jnp.bfloat16))
    cite_blocks = (
        jnp.dot(paper_features, cite_weight, preferred_element_type=jnp.float32)
        .astype(jnp.bfloat16)
        .reshape(block_total, tile_size, feat_out)
    )
    outgoing = cite_blocks[asked_blocks].reshape(wide_size, slot_cap, tile_size, feat_out)
    incoming = lax.all_to_all(outgoing, "wide", split_axis=0, concat_axis=0, tiled=True).reshape(
        slot_total, tile_size, feat_out
    )
    sender_rows = incoming[slot_index]
    message_product = jnp.einsum(
        "hpb,hbo->hpo", masked_values, sender_rows, preferred_element_type=jnp.float32
    )
    target_hot_flags = (
        tile_target_block[:, None] == jnp.arange(block_total, dtype=jnp.int32)[None, :]
    ).astype(jnp.float32)
    summed_messages = jnp.einsum(
        "yq,ycg->qcg", target_hot_flags, message_product, precision=lax.Precision.HIGHEST
    )
    row_weight = jnp.sum(masked_values.astype(jnp.float32), axis=2)
    degree = jnp.einsum("tb,tr->br", target_hot_flags, row_weight, precision=lax.Precision.HIGHEST)
    inverse = 1.0 / jnp.maximum(degree, 1.0)
    cite_mix = (summed_messages * inverse[..., None]).reshape(row_total, feat_out)
    hot_table = lax.all_gather(hot_embed.astype(jnp.bfloat16), "hot", axis=0, tiled=True)
    hot_total = hot_table.shape[0]
    author_iota = jnp.arange(hot_total, dtype=jnp.int32)[None, :]
    counts = jnp.zeros((row_total, hot_total), jnp.float32)
    for author_slot in range(HK):
        counts = counts + (hot_ids[:, author_slot : author_slot + 1] == author_iota).astype(
            jnp.float32
        )
    counts_low = counts.astype(jnp.bfloat16)
    author_mix = jnp.dot(counts_low, hot_table, preferred_element_type=jnp.float32) / HK
    preact = (
        jnp.dot(paper_features, self_weight, preferred_element_type=jnp.float32)
        + cite_mix
        + author_mix
    )
    sigmoid_pre = jax.nn.sigmoid(preact)
    hidden = (preact * sigmoid_pre).astype(jnp.bfloat16)
    gradient = cotangent.astype(jnp.float32) * sigmoid_pre * (1.0 + preact * (1.0 - sigmoid_pre))
    pre_grad = gradient.astype(jnp.bfloat16)
    self_local = lax.dot_general(
        paper_features, pre_grad, (((0,), (0,)), ((), ())), preferred_element_type=jnp.float32
    )
    scaled_messages = (
        pre_grad.astype(jnp.float32).reshape(block_total, tile_size, feat_out) * inverse[..., None]
    ).astype(jnp.bfloat16)
    backward_product = jnp.einsum(
        "yvs,yvo->yso",
        masked_values,
        scaled_messages[tile_target_block],
        preferred_element_type=jnp.float32,
    ).astype(jnp.bfloat16)
    outgoing_back = jnp.einsum(
        "ts,tcf->scf",
        placement.astype(jnp.bfloat16),
        backward_product,
        preferred_element_type=jnp.float32,
    ).astype(jnp.bfloat16)
    returned = lax.all_to_all(
        outgoing_back.reshape(wide_size, slot_cap, tile_size, feat_out),
        "wide",
        split_axis=0,
        concat_axis=0,
        tiled=True,
    ).reshape(slot_total, tile_size, feat_out)
    asked_hot = (asked_blocks[:, None] == jnp.arange(block_total, dtype=jnp.int32)[None, :]).astype(
        jnp.bfloat16
    )
    block_grad = jnp.einsum(
        "sb,scf->bcf", asked_hot, returned, preferred_element_type=jnp.float32
    ).reshape(row_total, feat_out)
    cite_local = lax.dot_general(
        paper_features.astype(jnp.float32),
        block_grad,
        (((0,), (0,)), ((), ())),
        precision=lax.Precision.HIGHEST,
    )
    self_share, cite_share = (
        lax.psum_scatter(self_local, "wide", scatter_dimension=0, tiled=True),
        lax.psum_scatter(cite_local, "wide", scatter_dimension=0, tiled=True),
    )
    self_grad, cite_grad = lax.psum((self_share, cite_share), "hot")
    author_local = (
        lax.dot_general(
            counts_low, pre_grad, (((0,), (0,)), ((), ())), preferred_element_type=jnp.float32
        )
        / HK
    )
    own_count = hot_embed.shape[0]
    total_rows = lax.psum(author_local, ("wide", "hot"))
    own_rows = lax.dynamic_slice_in_dim(total_rows, lax.axis_index("hot") * own_count, own_count, 0)
    return (hidden, self_grad, cite_grad, own_rows)


def solution(mesh):
    return jax.shard_map(
        on_device,
        mesh=mesh,
        in_specs=(
            P(("wide", "hot"), None),
            P(),
            P(),
            P("hot", None),
            P(("wide", "hot"), None),
            P(("wide", "hot"), None, None),
            P(("wide", "hot")),
            P(("wide", "hot")),
            P(("wide", "hot")),
            P(("wide", "hot")),
            P(("wide", "hot"), None),
        ),
        out_specs=(P(("wide", "hot"), None), P("wide", None), P("wide", None), P("hot", None)),
        check_vma=False,
    )
```

profile of v0, /device:TPU:32, one launch (start us, length us, event | category | flops | bytes accessed | tf_op | source)
XLA Modules:
  0.0 1109.6 jit_solution(8807699122357178833)
XLA Ops:
  7.2 0.0 copy-start
  7.2 0.8 fusion.16
  8.0 0.1 reduce_window_sum.11
  8.1 0.8 select_reduce_fusion.1
  8.9 0.7 compare_select_fusion.1
  9.6 0.7 select_reduce_fusion
  10.3 0.7 copy.40
  11.0 18.2 %all-to-all-start = ((s32[64,1,1]{2,1,0:T(1,128)}), s32[64,1,1]{2,1,0:T(1,128)S(1)}, u32[]{:S(2)}, u32[]{:S(2)}) async-start(s32[64,1,1]{2,1,0:T(1,128)} %copy.40), calls=%async_computation | async-start | bytes 65536 | tf_op jit(solution)/shard_map/all_to_all | solution.py:38
  29.3 0.0 copy-done
  29.3 1.6 convolution_convert_fusion.1
  30.9 12.0 %all-to-all-done = s32[64,1,1]{2,1,0:T(1,128)S(1)} async-done(((s32[64,1,1]{2,1,0:T(1,128)}), s32[64,1,1]{2,1,0:T(1,128)S(1)}, u32[]{:S(2)}, u32[]{:S(2)}) %all-to-all-start) | async-done | bytes 288 | tf_op jit(solution)/shard_map/all_to_all | solution.py:38
  42.8 1.2 reduce
  44.1 2.8 gather_fusion
  46.9 0.0 copy-start.5
  46.9 6.6 all-to-all-start.1
  53.5 0.0 copy-done.4
  53.5 0.0 copy-done.7
  53.5 0.1 iota_compare_fusion.10
  53.6 0.0 copy-done.1
  53.6 1.0 convert_reduce_fusion
  54.7 0.0 copy-done.6
  54.7 0.1 fusion.10
  54.8 0.1 copy.42
  55.0 0.0 copy-done.5
  55.0 13.8 %all_gather.3 = bf16[1024,256]{1,0:T(8,128)(2,1)S(1)} all-gather(bf16[128,256]{1,0:T(8,128)(2,1)S(1)} %convert_element_type.75), channel_id=1, replica_groups=mesh['wide'=64,'hot'=8] {'hot'}, dimensions={0}, use_global_device_ids=true | all-gather | bytes 589824 | tf_op jit(solution)/shard_map/all_gather | solution.py:66
  68.8 6.4 convolution_multiply_fusion.1
  75.2 165.2 %all-to-all-done.1 = bf16[64,1,128,256]{3,2,1,0:T(8,128)(2,1)} async-done(((bf16[64,1,128,256]{3,2,1,0:T(8,128)(2,1)}), bf16[64,1,128,256]{3,2,1,0:T(8,128)(2,1)}, u32[]{:S(2)}, u32[]{:S(2)}) %all-to-all-start.1) | async-done | bytes 4194336 | tf_op jit(solution)/shard_map/all_to_all | solution.py:49
  240.4 4.2 gather_fusion.1
  244.6 2.2 fusion.12
  246.8 0.0 copy-start.8
  246.8 0.0 copy-start.9
  246.8 0.0 copy-start.10
  246.8 3.9 fusion.6
  250.7 0.3 copy.43
  251.1 0.0 copy-done.8
  251.1 1.7 multiply_convert_fusion
  252.8 0.1 convert.1
  252.9 0.6 fusion.11
  253.5 0.1 copy-done.2
  253.6 0.1 copy.45
  253.7 2.0 gather_fusion.2
  255.7 3.3 convolution_convert_fusion
  259.0 1.6 convert_bitcast_fusion
  260.6 4.4 copy.48
  265.0 8.3 all-to-all-start.2
  273.3 0.0 all-reduce.7.cloned.1.call-start
  273.4 0.0 copy-done.3
  273.4 5.4 convolution_multiply_fusion
  278.8 0.0 all-reduce.7.cloned.1.call-update
  278.8 0.3 all-reduce.9.cloned.1.call-start
  279.1 1.5 convolution_bitcast_fusion.1
  280.6 183.3 %all-to-all-done.2 = bf16[64,1,128,256]{3,2,1,0:T(8,128)(2,1)} async-done(((bf16[64,1,128,256]{3,2,1,0:T(8,128)(2,1)}), bf16[64,1,128,256]{3,2,1,0:T(8,128)(2,1)}, u32[]{:S(2)}, u32[]{:S(2)}) %all-to-all-start.2) | async-done | bytes 4194336 | tf_op jit(solution)/shard_map/all_to_all | solution.py:103
  464.0 4.5 fusion
  468.5 0.3 copy.50
  468.8 2.4 convolution_bitcast_fusion
  471.2 0.0 all-reduce.9.cloned.1.call-update
  471.3 1.3 dynamic-slice
  473.2 323.1 %all-reduce.7.cloned.1.call-done = f32[1024,256]{1,0:T(8,128)} async-done(((f32[1024,256]{1,0:T(8,128)}), f32[1024,256]{1,0:T(8,128)}) %all-reduce.7.cloned.1.call-update) | async-done | bytes 1048592 | tf_op jit(solution)/shard_map/psum | solution.py:134
  796.3 1.6 constant_dynamic-slice_fusion.2
  797.9 276.0 %all-reduce.9.cloned.1.call-done = (f32[768,256]{0,1:T(8,128)}, f32[768,256]{0,1:T(8,128)}) async-done(((f32[768,256]{0,1:T(8,128)}, f32[768,256]{0,1:T(8,128)}), (f32[768,256]{0,1:T(8,128)}, f32[768,256]{0,1:T(8,128)})) %all-reduce.9.cloned.1.call-update) | async-done | bytes 1572880
  1073.9 1.2 constant_dynamic-slice_fusion
  1075.1 26.3 %all-reduce.3 = (f32[12,256]{0,1:T(8,128)S(1)}, f32[12,256]{0,1:T(8,128)S(1)}) all-reduce(f32[12,256]{0,1:T(8,128)S(1)} %get-tuple-element.37, f32[12,256]{0,1:T(8,128)S(1)} %get-tuple-element.36), channel_id=1, replica_groups=mesh['wide'=64,'hot'=8] {'hot'}, use_global_device_ids=true, to_apply=%region_5.6 | all-reduce | flops 6144 | bytes 49152 | tf_op jit(solution)/shard_map/psum | solution.py:126
  1101.3 0.7 copy.51
  1102.0 0.7 copy.52
  (15 shorter events, 0.1 us)
Async XLA Ops:
  7.2 22.1 %copy-start = (bf16[1024,768]{1,0:T(8,128)(2,1)S(1)}, bf16[1024,768]{1,0:T(8,128)(2,1)}, u32[]{:S(2)}) copy-start(bf16[1024,768]{1,0:T(8,128)(2,1)} %param.11) | copy-start | bytes 4718596
  11.0 31.8 %all-to-all-start = ((s32[64,1,1]{2,1,0:T(1,128)}), s32[64,1,1]{2,1,0:T(1,128)S(1)}, u32[]{:S(2)}, u32[]{:S(2)}) async-start(s32[64,1,1]{2,1,0:T(1,128)} %copy.40), calls=%async_computation | async-start | bytes 65536 | tf_op jit(solution)/shard_map/all_to_all | solution.py:38
  46.9 6.6 copy-start.4
  46.9 6.7 copy-start.7
  46.9 6.7 copy-start.1
  46.9 7.8 copy-start.6
  46.9 8.1 copy-start.5
  46.9 193.5 %all-to-all-start.1 = ((bf16[64,1,128,256]{3,2,1,0:T(8,128)(2,1)}), bf16[64,1,128,256]{3,2,1,0:T(8,128)(2,1)}, u32[]{:S(2)}, u32[]{:S(2)}) async-start(bf16[64,1,128,256]{3,2,1,0:T(8,128)(2,1)} %bitcast.57), calls=%async_computation.1 | async-start | bytes 8388608 | tf_op jit(solution)/shard_map/all_to_all | solution.py:49
  246.8 4.3 copy-start.8
  246.8 4.3 copy-start.9
  246.8 4.3 copy-start.10
  252.8 0.8 copy-start.2
  265.0 8.3 copy-start.3
  265.0 198.9 %all-to-all-start.2 = ((bf16[64,1,128,256]{3,2,1,0:T(8,128)(2,1)}), bf16[64,1,128,256]{3,2,1,0:T(8,128)(2,1)}, u32[]{:S(2)}, u32[]{:S(2)}) async-start(bf16[64,1,128,256]{3,2,1,0:T(8,128)(2,1)} %copy.48), calls=%async_computation.2 | async-start | bytes 8388608 | tf_op jit(solution)/shard_map/all_to_all | solution.py:103
  273.3 523.0 %all-reduce.7.cloned.1.call-start = ((), (), s32[]{:S(2)}) async-start(), calls=%async_computation.3 | async-start | bytes 2097152 | tf_op jit(solution)/shard_map/psum | solution.py:134
  278.8 795.1 %all-reduce.9.cloned.1.call-start = ((), (), s32[]{:S(2)}) async-start(), calls=%async_computation.4 | async-start | bytes 3145728
Sparse Core Ops, SparseCore 0:
  279.6 516.6 all-reduce.6
  799.8 274.0 all-reduce.8
where the time goes:
time: 1110 us
  waiting for transfers between devices  960 us (86%)
  blocking collectives  40.1 us (4%)
  matrix products  34.6 us (3%)
  starting transfers between devices  33.4 us (3%)
  local copies, waits for them, and re-layouts  20.6 us (2%)
  between operations  15 us (1%)
    psum x1, waiting for transfers between devices, on_device(): total_rows = lax.psum(author_local, ('wide', 'hot'))  323 us
    unnamed x3, waiting for transfers between devices  276 us
    all_to_all x1, waiting for transfers between devices, on_device(): lax.all_to_all(outgoing_back.reshape(wide_size, slot_cap, tile_size, feat...  183 us
    all_to_all x1, waiting for transfers between devices, on_device(): lax.all_to_all(outgoing, 'wide', split_axis=0, concat_axis=0, tiled=True)  165 us
    psum x1, blocking collectives, on_device(): self_grad, cite_grad = lax.psum((self_share, cite_share), 'hot')  26.3 us
  transfers between devices with their start and end apart: 5, of which 5 were waited for; matrix products, arithmetic and copies ran while one was open for 2% of the time, Pallas kernels for 0%

commit v1 on v0

v1 whole, which is shorter than its diff:
```python
import functools

import jax
import jax.numpy as jnp
from jax import lax
from jax.experimental import pallas as pl
from jax.experimental.pallas import tpu as pltpu
from jax.sharding import PartitionSpec as P

HK = 8
BLOCKS = 8
NX = 4
SUBS = 4
PAD = 16
MESH = pl.DeviceIdType.MESH
F32 = jnp.float32
BF16 = jnp.bfloat16
VMEM_LIMIT = 58 * 1024 * 1024


def place(nz):
    w = lax.axis_index("wide")
    h = lax.axis_index("hot")
    return w // NX, w % NX, w, h


def greet(partners):
    barrier = pltpu.get_barrier_semaphore()
    for partner in partners:
        pl.semaphore_signal(barrier, inc=1, device_id=partner, device_id_type=MESH)
    return lambda: pl.semaphore_wait(barrier, len(partners))


def remote(src, dst, send, recv, target):
    return pltpu.make_async_remote_copy(
        src_ref=src, dst_ref=dst, send_sem=send, recv_sem=recv, device_id=target, device_id_type=MESH
    )


def forward_kernel(nz, nh, *refs):
    half = nz // 2
    (feat, w_cite, w_self, hot, ids, req) = refs[:6]
    (arrived, base, counts, table_out) = refs[6:10]
    refs = refs[10:]
    own, packed, table, asked = refs[:4]
    right = [own] + list(refs[4 : 4 + half])
    left = [own] + list(refs[4 + half : 3 + 2 * half]) + [right[half]]
    (r_send, r_recv, l_send, l_recv, x_send, x_recv, h_send, h_recv, q_send, q_recv, q_local) = refs[
        3 + 2 * half :
    ]
    z, x, w, h = place(nz)
    blocks, size, width = own.shape
    hot_rows = hot.shape[0]
    hot_total = table.shape[0]
    per = blocks // SUBS
    to_right = (lax.rem(z + 1, nz) * NX + x, h)
    to_left = (lax.rem(z + nz - 1, nz) * NX + x, h)
    x_peers = [(z * NX + lax.rem(x + d, NX), h) for d in range(1, NX)]
    h_peers = [(w, lax.rem(h + d, nh)) for d in range(1, nh)]
    wait_all = greet([to_right, to_left] + x_peers + h_peers)

    own[...] = (
        jnp.dot(feat[...], w_cite[...], preferred_element_type=F32)
        .astype(BF16)
        .reshape(blocks, size, width)
    )
    my_rows = pl.ds(pl.multiple_of(h * hot_rows, hot_rows), hot_rows)
    table[my_rows] = hot[...].astype(BF16)
    table_out[0] = req[...]
    wait_all()

    def ring(side, k, s):
        part = pl.ds(s * per, per)
        if side == "r":
            return remote(
                right[k - 1].at[part], right[k].at[part], r_send.at[k - 1, s], r_recv.at[k - 1, s], to_right
            )
        return remote(
            left[k - 1].at[part], left[k].at[part], l_send.at[k - 1, s], l_recv.at[k - 1, s], to_left
        )

    def goes(side, k, s):
        if k > half:
            return False
        return k < half or (s < SUBS // 2) == (side == "r")

    for s in range(SUBS):
        for side in "rl":
            if goes(side, 1, s):
                ring(side, 1, s).start()
    asks = []
    for d in range(1, NX):
        asks.append(
            remote(
                table_out.at[0], table_out.at[NX - d], q_send.at[d - 1], q_recv.at[NX - d - 1], x_peers[d - 1]
            )
        )
    for copy in asks:
        copy.start()
    hots = []
    for d in range(1, nh):
        hots.append(
            remote(
                table.at[my_rows], table.at[my_rows], h_send.at[d - 1], h_recv.at[nh - d - 1], h_peers[d - 1]
            )
        )
    for copy in hots:
        copy.start()
    for d in range(1, NX):
        remote(
            table_out.at[0], table_out.at[d], q_send.at[d - 1], q_recv.at[d - 1], x_peers[d - 1]
        ).wait_recv()
    local = pltpu.make_async_copy(table_out, asked, q_local)
    local.start()
    local.wait()

    def exchange(zoff, source):
        owner = lax.rem(z + zoff, nz) * NX + x
        for d in range(1, NX):
            packed[d - 1, zoff] = source[jnp.maximum(asked[d, 0, owner], 0)]
            remote(
                packed.at[d - 1, zoff],
                arrived.at[NX - d, zoff],
                x_send.at[d - 1, zoff],
                x_recv.at[NX - d - 1, zoff],
                x_peers[d - 1],
            ).start()
        arrived[0, zoff] = source[jnp.maximum(asked[0, 0, owner], 0)]

    def rows_of(i):
        rows = pl.ds(i * size, size)
        authors = lax.broadcasted_iota(jnp.int32, (size, hot_total), 1)
        many = jnp.zeros((size, hot_total), F32)
        for k in range(HK):
            many = many + jnp.where(ids[rows, k : k + 1] == authors, 1.0, 0.0)
        many = many.astype(BF16)
        counts[rows] = many
        base[rows] = jnp.dot(feat[rows], w_self[...], preferred_element_type=F32) + jnp.dot(
            many, table[...], preferred_element_type=F32
        ) * (1.0 / HK)

    exchange(0, own)
    for k in range(1, half + 1):
        for s in range(SUBS):
            for side in "rl":
                if goes(side, k, s):
                    ring(side, k, s).wait_recv()
                if goes(side, k + 1, s):
                    ring(side, k + 1, s).start()
        exchange(nz - k, right[k])
        if k < half:
            exchange(k, left[k])
        if k == 1:
            for d in range(1, nh):
                there = pl.ds(pl.multiple_of(lax.rem(h + d, nh) * hot_rows, hot_rows), hot_rows)
                remote(
                    table.at[there], table.at[there], h_send.at[d - 1], h_recv.at[d - 1], h_peers[d - 1]
                ).wait_recv()
        for i in range(blocks):
            if i * half // blocks == k - 1:
                rows_of(i)
    for zoff in range(nz):
        for d in range(1, NX):
            copy = remote(
                packed.at[d - 1, zoff],
                arrived.at[d, zoff],
                x_send.at[d - 1, zoff],
                x_recv.at[d - 1, zoff],
                x_peers[d - 1],
            )
            copy.wait_recv()
            copy.wait_send()
    for copy in asks + hots:
        copy.wait_send()
    for k in range(1, half + 1):
        for s in range(SUBS):
            for side in "rl":
                if goes(side, k, s):
                    ring(side, k, s).wait_send()


def forward(nz, nh, feat, w_cite, w_self, hot, ids, req):
    half = nz // 2
    rows, width = feat.shape[0], w_self.shape[1]
    size = rows // BLOCKS
    blocks = rows // size
    hot_total = hot.shape[0] * nh
    vmem = pl.BlockSpec(memory_space=pltpu.VMEM)
    chunk = (blocks, size, width)
    dma = pltpu.SemaphoreType.DMA
    return pl.pallas_call(
        functools.partial(forward_kernel, nz, nh),
        out_shape=(
            jax.ShapeDtypeStruct((NX, nz, size, width), BF16),
            jax.ShapeDtypeStruct((rows, width), F32),
            jax.ShapeDtypeStruct((rows, hot_total), BF16),
            jax.ShapeDtypeStruct((NX, 8, req.shape[1]), jnp.int32),
        ),
        in_specs=[vmem] * 6,
        out_specs=(vmem,) * 4,
        scratch_shapes=[
            pltpu.VMEM(chunk, BF16),
            pltpu.VMEM((NX - 1, nz, size, width), BF16),
            pltpu.VMEM((hot_total, width), BF16),
            pltpu.SMEM((NX, 8, req.shape[1]), jnp.int32),
        ]
        + [pltpu.VMEM(chunk, BF16)] * (2 * half - 1)
        + [
            dma((half, SUBS)),
            dma((half, SUBS)),
            dma((half, SUBS)),
            dma((half, SUBS)),
            dma((NX - 1, nz)),
            dma((NX - 1, nz)),
            dma((nh - 1,)),
            dma((nh - 1,)),
            dma((NX - 1,)),
            dma((NX - 1,)),
            dma,
        ],
        compiler_params=pltpu.CompilerParams(
            collective_id=1, has_side_effects=True, vmem_limit_bytes=VMEM_LIMIT
        ),
    )(feat, w_cite, w_self, hot, ids, req)


def local_kernel(
    slots, used, target, arrived, values, base, cotangent, hidden, grad, back, total, masked, scaled, inverse
):
    tiles, size, _ = values.shape
    width = base.shape[1]
    blocks = total.shape[0]
    total[...] = jnp.zeros_like(total)
    ones = jnp.ones((size, size), BF16)
    row = lax.broadcasted_iota(jnp.int32, (size, size), 0)

    def message(t, carry):
        m = jnp.where(row < used[t], values[t].astype(F32), 0.0).astype(BF16)
        masked[t] = m
        there = target[t]
        total[there, :, :width] += jnp.dot(m, arrived[slots[t]], preferred_element_type=F32)
        total[there, :, width:] += jnp.dot(m, ones, preferred_element_type=F32)
        return carry

    lax.fori_loop(0, tiles, message, 0)

    def finish(j, carry):
        rows = pl.ds(pl.multiple_of(j * size, size), size)
        inv = 1.0 / jnp.maximum(total[j, :, width : width + 1], 1.0)
        pre = base[rows] + total[j, :, :width] * inv
        s = jax.nn.sigmoid(pre)
        hidden[rows] = (pre * s).astype(BF16)
        g = (cotangent[rows].astype(F32) * s * (1.0 + pre * (1.0 - s))).astype(BF16)
        grad[rows] = g
        scaled[j] = (g.astype(F32) * inv).astype(BF16)
        return carry

    lax.fori_loop(0, blocks, finish, 0)

    def backward(t, carry):
        back[t] = lax.dot_general(
            masked[t], scaled[target[t]], (((0,), (0,)), ((), ())), preferred_element_type=F32
        ).astype(BF16)
        return carry

    lax.fori_loop(0, tiles, backward, 0)


def local_part(slots, used, target, arrived, values, base, cotangent):
    tiles, size, _ = values.shape
    rows, width = base.shape
    blocks = rows // size
    vmem = pl.BlockSpec(memory_space=pltpu.VMEM)
    smem = pl.BlockSpec(memory_space=pltpu.SMEM)
    return pl.pallas_call(
        local_kernel,
        out_shape=(
            jax.ShapeDtypeStruct((rows, width), BF16),
            jax.ShapeDtypeStruct((rows, width), BF16),
            jax.ShapeDtypeStruct((tiles, size, width), BF16),
        ),
        in_specs=[smem] * 3 + [vmem] * 4,
        out_specs=(vmem,) * 3,
        scratch_shapes=[
            pltpu.VMEM((blocks, size, width + size), F32),
            pltpu.VMEM((tiles, size, size), BF16),
            pltpu.VMEM((blocks, size, width), BF16),
            pltpu.VMEM((8, 128), F32),
        ],
        compiler_params=pltpu.CompilerParams(vmem_limit_bytes=VMEM_LIMIT),
    )(slots, used, target, arrived, values, base, cotangent)


class WeightSum:
    def __init__(self, where, nz, nh, refs):
        self.z, self.x, self.w, self.h = where
        self.nz, self.nh = nz, nh
        (self.mine, self.got1, self.mid, self.got2, self.last, self.got3, self.done) = refs[:7]
        (self.s1, self.r1, self.s2, self.r2, self.s3, self.r3, self.s4, self.r4) = refs[7:15]
        self.share = self.mine.shape[1] // NX

    @staticmethod
    def scratch(nz, nh, share, width, kind):
        dma = pltpu.SemaphoreType.DMA
        two = nz // nh
        return [
            pltpu.VMEM((nz, NX * share, width), kind),
            pltpu.VMEM((nh - 1, two, NX * share, width), kind),
            pltpu.VMEM((NX, two, PAD, width), F32),
            pltpu.VMEM((NX - 1, two, PAD, width), F32),
            pltpu.VMEM((two, PAD, width), F32),
            pltpu.VMEM((nz - 1, PAD, width), F32),
            pltpu.VMEM((PAD, width), F32),
            dma((nh - 1, two)),
            dma((nh - 1, two)),
            dma((NX - 1,)),
            dma((NX - 1,)),
            dma((two,)),
            dma((nz - 1,)),
            dma((nh - 1,)),
            dma,
        ]

    def copies1(self):
        out = []
        for d in range(1, self.nh):
            peer = lax.rem(self.h + d, self.nh)
            for i in range(self.nz // self.nh):
                e = self.nh - d - 1
                out.append(
                    remote(
                        self.mine.at[peer + i * self.nh],
                        self.got1.at[e, i],
                        self.s1.at[d - 1, i],
                        self.r1.at[e, i],
                        (self.w, peer),
                    )
                )
        return out

    def copies2(self):
        out = []
        for d in range(1, NX):
            peer = lax.rem(self.x + d, NX)
            e = NX - d - 1
            out.append(
                remote(
                    self.mid.at[peer],
                    self.got2.at[e],
                    self.s2.at[d - 1],
                    self.r2.at[e],
                    (self.z * NX + peer, self.h),
                )
            )
        return out

    def each3(self, act):
        for i in range(self.nz // self.nh):
            there = self.h + i * self.nh
            off = lax.rem(self.z - there + self.nz, self.nz)

            @pl.when(off != 0)
            def _():
                act(
                    remote(
                        self.last.at[i],
                        self.got3.at[off - 1],
                        self.s3.at[i],
                        self.r3.at[off - 1],
                        (there * NX + self.x, self.h),
                    )
                )

    def copies4(self):
        return [
            remote(
                self.done, self.done, self.s4.at[d - 1], self.r4, (self.w, lax.rem(self.h + d, self.nh))
            )
            for d in range(1, self.nh)
        ]

    def stage1(self):
        for copy in self.copies1():
            copy.start()

    def stage2(self):
        self.mid[...] = jnp.zeros_like(self.mid)
        for copy in self.copies1():
            copy.wait_recv()
        for i in range(self.nz // self.nh):
            sums = self.mine[self.h + i * self.nh].astype(F32)
            for e in range(self.nh - 1):
                sums = sums + self.got1[e, i].astype(F32)
            for peer in range(NX):
                self.mid[peer, i, : self.share] = sums[peer * self.share : (peer + 1) * self.share]
        for copy in self.copies2():
            copy.start()

    def stage3(self):
        for copy in self.copies2():
            copy.wait_recv()
        sums = self.mid[self.x]
        for e in range(NX - 1):
            sums = sums + self.got2[e]
        self.last[...] = sums
        self.each3(lambda copy: copy.start())

    def stage4(self):
        @pl.when(lax.rem(self.z, self.nh) == self.h)
        def _():
            for o in range(self.nz - 1):
                remote(
                    self.last.at[0], self.got3.at[o], self.s3.at[0], self.r3.at[o], (self.w, self.h)
                ).wait_recv()
            sums = self.last[self.z // self.nh]
            for o in range(self.nz - 1):
                sums = sums + self.got3[o]
            self.done[...] = sums
            for copy in self.copies4():
                copy.start()

    def finish(self, out):
        @pl.when(lax.rem(self.z, self.nh) != self.h)
        def _():
            self.copies4()[0].wait_recv()

        out[...] = self.done[: self.share]

    def drain(self):
        for copy in self.copies1() + self.copies2():
            copy.wait_send()
        self.each3(lambda copy: copy.wait_send())

        @pl.when(lax.rem(self.z, self.nh) == self.h)
        def _():
            for copy in self.copies4():
                copy.wait_send()


class AuthorSum:
    def __init__(self, where, nz, nh, refs):
        self.z, self.x, self.w, self.h = where
        self.nz, self.nh, self.np = nz, nh, nz // 2
        (self.mine, self.got1, self.mid, self.got2, self.cut, self.got3, self.sums4, self.rows5) = refs[:8]
        (self.s1, self.r1, self.s2, self.r2, self.s3, self.r3, self.s4, self.r4, self.s5, self.r5) = refs[8:18]

    @staticmethod
    def scratch(nz, nh, rows, width):
        dma = pltpu.SemaphoreType.DMA
        part = rows // NX
        pieces = nz // 2
        return [
            pltpu.VMEM((nh, rows, width), F32),
            pltpu.VMEM((nh - 1, rows, width), F32),
            pltpu.VMEM((NX, part, width), F32),
            pltpu.VMEM((NX - 1, part, width), F32),
            pltpu.VMEM((pieces, 8, width // 2), F32),
            pltpu.VMEM((nz - 1, 8, width // 2), F32),
            pltpu.VMEM((pieces, 8, width // 2), F32),
            pltpu.VMEM((NX, part, width), F32),
            dma((nh - 1,)),
            dma((nh - 1,)),
            dma((NX - 1,)),
            dma((NX - 1,)),
            dma((nz - 1,)),
            dma((nz - 1,)),
            dma((pieces - 1,)),
            dma((pieces - 1,)),
            dma((NX - 1,)),
            dma((NX - 1,)),
        ]

    def copies1(self):
        out = []
        for d in range(1, self.nh):
            peer = lax.rem(self.h + d, self.nh)
            e = self.nh - d - 1
            out.append(
                remote(self.mine.at[peer], self.got1.at[e], self.s1.at[d - 1], self.r1.at[e], (self.w, peer))
            )
        return out

    def copies2(self):
        out = []
        for d in range(1, NX):
            peer = lax.rem(self.x + d, NX)
            e = NX - d - 1
            to = (self.z * NX + peer, self.h)
            out.append(remote(self.mid.at[peer], self.got2.at[e], self.s2.at[d - 1], self.r2.at[e], to))
        return out

    def copies3(self):
        out = []
        for d in range(1, self.nz):
            peer = lax.rem(self.z + d, self.nz)
            e = self.nz - d - 1
            to = (peer * NX + self.x, self.h)
            out.append(
                remote(
                    self.cut.at[lax.rem(peer, self.np)], self.got3.at[e], self.s3.at[d - 1], self.r3.at[e], to
                )
            )
        return out

    def copies4(self, coming=False):
        out = []
        p = lax.rem(self.z, self.np)
        for d in range(1, self.np):
            other = lax.rem(p + d, self.np)
            to = ((self.z - p + other) * NX + self.x, self.h)
            e = d - 1 if coming else self.np - d - 1
            piece = self.sums4.at[other if coming else p]
            out.append(remote(piece, piece, self.s4.at[d - 1], self.r4.at[e], to))
        return out

    def copies5(self, coming=False):
        out = []
        for d in range(1, NX):
            peer = lax.rem(self.x + d, NX)
            e = d - 1 if coming else NX - d - 1
            rows = self.rows5.at[peer if coming else self.x]
            out.append(remote(rows, rows, self.s5.at[d - 1], self.r5.at[e], (self.z * NX + peer, self.h)))
        return out

    def stage1(self):
        for copy in self.copies1():
            copy.start()

    def stage2(self):
        for copy in self.copies1():
            copy.wait_recv()
        sums = self.mine[self.h]
        for e in range(self.nh - 1):
            sums = sums + self.got1[e]
        self.mid[...] = sums.reshape(self.mid.shape)
        for copy in self.copies2():
            copy.start()

    def stage3(self):
        for copy in self.copies2():
            copy.wait_recv()
        sums = self.mid[self.x]
        for e in range(NX - 1):
            sums = sums + self.got2[e]
        lanes = self.cut.shape[2]
        for p in range(self.np):
            g, c = p // 2, p % 2
            self.cut[p] = sums[g * 8 : (g + 1) * 8, c * lanes : (c + 1) * lanes]
        for copy in self.copies3():
            copy.start()

    def stage4(self):
        for copy in self.copies3():
            copy.wait_recv()
        p = lax.rem(self.z, self.np)
        sums = self.cut[p]
        for e in range(self.nz - 1):
            sums = sums + self.got3[e]
        self.sums4[p] = sums
        for copy in self.copies4():
            copy.start()

    def stage5(self):
        for copy in self.copies4(True):
            copy.wait_recv()
        lanes = self.cut.shape[2]
        for p in range(self.np):
            g, c = p // 2, p % 2
            self.rows5[self.x, g * 8 : (g + 1) * 8, c * lanes : (c + 1) * lanes] = self.sums4[p]
        for copy in self.copies5():
            copy.start()

    def finish(self, out):
        for copy in self.copies5(True):
            copy.wait_recv()
        out[...] = self.rows5[...].reshape(out.shape)

    def drain(self):
        for copy in self.copies1() + self.copies2() + self.copies3() + self.copies4() + self.copies5():
            copy.wait_send()


def backward_kernel(nz, nh, *refs):
    half = nz // 2
    (tile_at, asked, back, feat, counts, grad) = refs[:6]
    (self_out, cite_out, author_out) = refs[6:9]
    refs = list(refs[9:])
    packed, came, far, near = refs[:4]
    refs = refs[4:]
    right, left = refs[:half], refs[half : 2 * half]
    (r_send, r_recv, l_send, l_recv, x_send, x_recv) = refs[2 * half : 2 * half + 6]
    refs = refs[2 * half + 6 :]
    where = place(nz)
    z, x, w, h = where
    selfs = WeightSum(where, nz, nh, refs[:15])
    cites = WeightSum(where, nz, nh, refs[15:30])
    authors = AuthorSum(where, nz, nh, refs[30:48])
    blocks, size, width = far.shape
    per = blocks // SUBS
    to_right = (lax.rem(z + 1, nz) * NX + x, h)
    to_left = (lax.rem(z + nz - 1, nz) * NX + x, h)
    z_peers = [(lax.rem(z + d, nz) * NX + x, h) for d in range(1, nz)]
    x_peers = [(z * NX + lax.rem(x + d, NX), h) for d in range(1, NX)]
    h_peers = [(w, lax.rem(h + d, nh)) for d in range(1, nh)]
    greet(z_peers + x_peers + h_peers)()

    def exchange(zoff):
        there = lax.rem(z + zoff, nz) * NX
        out = []
        for d in range(1, NX):
            packed[d - 1, zoff] = back[tile_at[there + lax.rem(x + d, NX)]]
            remote(
                packed.at[d - 1, zoff],
                came.at[NX - d - 1, zoff],
                x_send.at[d - 1, zoff],
                x_recv.at[NX - d - 1, zoff],
                x_peers[d - 1],
            ).start()

    def exchanged(zoff, what):
        for d in range(1, NX):
            copy = remote(
                packed.at[d - 1, zoff],
                came.at[d - 1, zoff],
                x_send.at[d - 1, zoff],
                x_recv.at[d - 1, zoff],
                x_peers[d - 1],
            )
            what(copy)

    step_rows = min(size, 32)

    def add_local(dst, sources, s, zoff):
        owner = lax.rem(z + zoff, nz) * NX + x
        wanted = [asked[d, 0, owner] for d in range(NX)]
        mine = tile_at[owner]

        def body(i, carry):
            rows = pl.ds(pl.multiple_of(i * step_rows, step_rows), step_rows)
            terms = [back[mine, rows].astype(F32)]
            for d in range(1, NX):
                terms.append(came[d - 1, zoff, rows].astype(F32))
            for j in range(s * per, (s + 1) * per):
                total = None
                for d in range(NX):
                    term = jnp.where(wanted[d] == j, terms[d], 0.0)
                    total = term if total is None else total + term
                for source in sources:
                    total = total + source[j, rows].astype(F32)
                dst[j, rows] = total.astype(BF16)
            return carry

        lax.fori_loop(0, size // step_rows, body, 0)

    def ring(side, k, s):
        part = pl.ds(s * per, per)
        bufs, send, recv, to = (
            (right, r_send, r_recv, to_right) if side == "r" else (left, l_send, l_recv, to_left)
        )
        src = far if k == half else bufs[k]
        return remote(src.at[part], bufs[k - 1].at[part], send.at[k - 1, s], recv.at[k - 1, s], to)

    def goes(side, k, s):
        return k < half or (s < SUBS // 2) == (side == "r")

    def product(lhs, rhs, put, step):
        def body(i, carry):
            at = pl.multiple_of(i * step, step)
            put(
                at,
                lax.dot_general(
                    lhs[:, pl.ds(at, step)], rhs[...], (((0,), (0,)), ((), ())), preferred_element_type=F32
                ),
            )
            return carry

        lax.fori_loop(0, lhs.shape[1] // step, body, 0)

    def put_weight(dest):
        group = dest.mine.shape[1]

        def put(at, value):
            first = at // group
            for i in range(value.shape[0] // group):
                dest.mine[first + i] = value[i * group : (i + 1) * group].astype(dest.mine.dtype)

        return put

    group = selfs.mine.shape[1]
    weight_step = group * 8 if feat.shape[1] % 128 == 0 else feat.shape[1]

    def put_author(at, value):
        rows = authors.mine.shape[1]
        for i in range(value.shape[0] // rows):
            authors.mine[at // rows + i] = value[i * rows : (i + 1) * rows] * (1.0 / HK)

    author_step = min(counts.shape[1], 256)

    def self_start():
        product(feat, grad, put_weight(selfs), weight_step)
        selfs.stage1()

    def author_start():
        product(counts, grad, put_author, author_step)
        authors.stage1()

    extras = [
        self_start,
        author_start,
        selfs.stage2,
        authors.stage2,
        selfs.stage3,
        authors.stage3,
        selfs.stage4,
        authors.stage4,
        authors.stage5,
        lambda: selfs.finish(self_out),
        lambda: authors.finish(author_out),
    ]

    exchange(half)
    exchange(half - 1)
    exchange(half + 1)
    for k in range(half, 0, -1):
        exchanged(k, lambda copy: copy.wait_recv())
        if k < half:
            exchanged(nz - k, lambda copy: copy.wait_recv())
        for s in range(SUBS):
            for side in "rl":
                if not goes(side, k, s):
                    continue
                bufs = right if side == "r" else left
                zoff = k if side == "r" else nz - k
                sources = []
                if k < half and goes(side, k + 1, s):
                    ring(side, k + 1, s).wait_recv()
                    sources = [bufs[k]]
                add_local(far if k == half else bufs[k], sources, s, zoff)
                ring(side, k, s).start()
        if k >= 2:
            exchange(k - 2)
            if k - 2 > 0:
                exchange(nz - k + 2)
        first = (half - k) * len(extras) // half
        last = (half - k + 1) * len(extras) // half
        for extra in extras[first:last]:
            extra()
    exchanged(0, lambda copy: copy.wait_recv())
    for s in range(SUBS):
        ring("r", 1, s).wait_recv()
        ring("l", 1, s).wait_recv()
        add_local(near, [right[0], left[0]], s, 0)

    def near_rows(at, step):
        return feat[:, pl.ds(at, step)]

    flat = near[...].reshape(blocks * size, width)

    def cite_body(i, carry):
        at = pl.multiple_of(i * weight_step, weight_step)
        put_weight(cites)(
            at,
            lax.dot_general(
                feat[:, pl.ds(at, weight_step)], flat, (((0,), (0,)), ((), ())), preferred_element_type=F32
            ),
        )
        return carry

    lax.fori_loop(0, feat.shape[1] // weight_step, cite_body, 0)
    cites.stage1()
    cites.stage2()
    cites.stage3()
    cites.stage4()
    for zoff in range(nz):
        exchanged(zoff, lambda copy: copy.wait_send())
    for k in range(half, 0, -1):
        for s in range(SUBS):
            for side in "rl":
                if goes(side, k, s):
                    ring(side, k, s).wait_send()
    selfs.drain()
    authors.drain()
    cites.finish(cite_out)
    cites.drain()


def backward(nz, nh, tile_at, asked, back, feat, counts, grad, share, hot_rows):
    half = nz // 2
    _, size, width = back.shape
    rows = feat.shape[0]
    chunk = (rows // size, size, width)
    vmem = pl.BlockSpec(memory_space=pltpu.VMEM)
    smem = pl.BlockSpec(memory_space=pltpu.SMEM)
    dma = pltpu.SemaphoreType.DMA
    return pl.pallas_call(
        functools.partial(backward_kernel, nz, nh),
        out_shape=(
            jax.ShapeDtypeStruct((share, width), F32),
            jax.ShapeDtypeStruct((share, width), F32),
            jax.ShapeDtypeStruct((hot_rows, width), F32),
        ),
        in_specs=[smem] * 2 + [vmem] * 4,
        out_specs=(vmem,) * 3,
        scratch_shapes=[
            pltpu.VMEM((NX - 1, nz, size, width), BF16),
            pltpu.VMEM((NX - 1, nz, size, width), BF16),
            pltpu.VMEM(chunk, BF16),
            pltpu.VMEM(chunk, BF16),
        ]
        + [pltpu.VMEM(chunk, BF16)] * (2 * half)
        + [
            dma((half, SUBS)),
            dma((half, SUBS)),
            dma((half, SUBS)),
            dma((half, SUBS)),
            dma((NX - 1, nz)),
            dma((NX - 1, nz)),
        ]
        + WeightSum.scratch(nz, nh, share, width, F32)
        + WeightSum.scratch(nz, nh, share, width, BF16)
        + AuthorSum.scratch(nz, nh, hot_rows, width),
        compiler_params=pltpu.CompilerParams(
            collective_id=2, has_side_effects=True, vmem_limit_bytes=VMEM_LIMIT
        ),
    )(tile_at, asked, back, feat, counts, grad)


def on_device(
    paper_features,
    self_weight,
    cite_weight,
    hot_embed,
    hot_ids,
    tile_values,
    tile_rows,
    tile_target_block,
    tile_block,
    tile_owner,
    cotangent,
):
    wide = lax.axis_size("wide")
    nh = lax.axis_size("hot")
    nz = wide // NX
    tiles = tile_values.shape[0]
    z, x, _, _ = place(nz)
    lanes = max(128, wide)
    owners = jnp.arange(lanes, dtype=jnp.int32)
    owned = tile_owner[:, None] == owners[None, :]
    numbers = jnp.arange(tiles, dtype=jnp.int32)
    wanted = jnp.max(jnp.where(owned, tile_block[:, None], -1), axis=0)
    tile_at = jnp.max(jnp.where(owned, numbers[:, None], 0), axis=0)
    req = jnp.broadcast_to(wanted[None, :], (8, lanes))
    slots = ((tile_owner % NX - x) % NX) * nz + (tile_owner // NX - z) % nz
    arrived, base, counts, asked = forward(
        nz, nh, paper_features, cite_weight, self_weight, hot_embed, hot_ids, req
    )
    _, _, size, width = arrived.shape
    hidden, grad, back = local_part(
        slots,
        tile_rows,
        tile_target_block,
        arrived.reshape(NX * nz, size, width),
        tile_values,
        base,
        cotangent,
    )
    self_grad, cite_grad, author_grad = backward(
        nz,
        nh,
        tile_at,
        asked,
        back,
        paper_features,
        counts,
        grad,
        self_weight.shape[0] // wide,
        hot_embed.shape[0],
    )
    return hidden, self_grad, cite_grad, author_grad


def solution(mesh):
    return jax.shard_map(
        on_device,
        mesh=mesh,
        in_specs=(
            P(("wide", "hot"), None),
            P(),
            P(),
            P("hot", None),
            P(("wide", "hot"), None),
            P(("wide", "hot"), None, None),
            P(("wide", "hot")),
            P(("wide", "hot")),
            P(("wide", "hot")),
            P(("wide", "hot")),
            P(("wide", "hot"), None),
        ),
        out_specs=(P(("wide", "hot"), None), P("wide", None), P("wide", None), P("hot", None)),
        check_vma=False,
    )
```

time: 1110 us -> 269 us (0.24)
  the two profiles are of different devices: /device:TPU:32 before, /device:TPU:17 now
where the time goes in v1:
time: 269 us; the launch traced here: 268 us
  Pallas kernels  259 us (96%)
  local copies, waits for them, and re-layouts  6.56 us (2%)
    pallas_call x1, Pallas kernels, backward(): pl.pallas_call(functools.partial(backward_kernel, nz, nh), out_shape=(jax...  132 us
    pallas_call x1, Pallas kernels, forward(): pl.pallas_call(functools.partial(forward_kernel, nz, nh), out_shape=(jax....  109 us
    pallas_call x1, Pallas kernels, local_part(): pl.pallas_call(local_kernel, out_shape=(jax.ShapeDtypeStruct((rows, width...  17.7 us
    unnamed x4, local copies, waits for them, and re-layouts  5.97 us

profile of v1, /device:TPU:17, one launch (start us, length us, event | category | flops | bytes accessed | tf_op | source)
XLA Modules:
  0.0 268.4 jit_solution(4283631958459377937)
XLA Ops:
  0.7 1.2 fusion.slots
  1.8 1.3 select_reduce_fusion
  3.1 0.6 broadcast_in_dim.32.refs_5_
  3.7 1.8 copy.16.refs_4_
  5.5 109.3 %shard_map.138 = (bf16[4,16,128,256]{3,2,1,0:T(8,128)(2,1)}, f32[1024,256]{1,0:T(8,128)}, bf16[1024,1024]{1,0:T(8,128)(2,1)}, s32[4,8,128]{2,1,0:T(8,128)}) custom-call(bf16[1024,768]{1,0:T(8,128)(2,1)} %refs_3_.3, bf16[768,256]{1,0:T(8,128)(2,1)} %refs_1_.1, bf16[768,256]{1,0:T(8,128)(2,1)} %refs_2_.1, f32[128,256]{1,0:T(8,128)} %refs_3_.2, ...), custom_call_target="tpu_custom_call" | custom-call | tf_op jit(solution)/shard_map/pallas_call | solution.py:191
  114.7 17.7 %shard_map.139 = (bf16[1024,256]{1,0:T(8,128)(2,1)}, bf16[1024,256]{1,0:T(8,128)(2,1)}, bf16[32,128,256]{2,1,0:T(8,128)(2,1)}) custom-call(s32[32]{0:T(128)} %fusion.slots, s32[32]{0:T(128)} %used.1, s32[32]{0:T(128)} %target.1, bf16[64,128,256]{2,1,0:T(8,128)(2,1)} %bitcast.1, bf16[32,128,128]{2,1,0:T(8,128)(2,1)} %values.1, ...), custom_call_target="tpu_custom_call" | custom-call | tf_op jit(solution)/shard_map/pallas_call | solution.py:275
  132.4 131.8 %shard_map.140 = (f32[12,256]{1,0:T(8,128)}, f32[12,256]{1,0:T(8,128)}, f32[128,256]{1,0:T(8,128)}) custom-call(s32[128]{0:T(128)} %get-tuple-element.24.refs_0_, s32[4,8,128]{2,1,0:T(8,128)} %get-tuple-element.17.refs_1_, bf16[32,128,256]{2,1,0:T(8,128)(2,1)} %get-tuple-element.18.refs_2_, bf16[1024,768]{1,0:T(8,128)(2,1)} %refs_3_.3, ...), custom_call_target="tpu_custom_call" | custom-call | tf_op jit(solution)/shard_map/pallas_call | solution.py:795
  264.2 1.3 copy.20
  265.5 1.3 copy.21
  266.8 1.6 copy.22

commit v2 on v1

v2 whole, which is shorter than its diff:
```python
import functools

import jax
import jax.numpy as jnp
from jax import lax
from jax.experimental import pallas as pl
from jax.experimental.pallas import tpu as pltpu
from jax.sharding import PartitionSpec as P

HK = 8
NX = 4
SUBS = 4
PAD = 16
MESH = pl.DeviceIdType.MESH
F32 = jnp.float32
BF16 = jnp.bfloat16
VMEM_LIMIT = 58 * 1024 * 1024


def place(nz):
    w = lax.axis_index("wide")
    h = lax.axis_index("hot")
    return w // NX, w % NX, w, h


def greet(partners):
    barrier = pltpu.get_barrier_semaphore()
    for partner in partners:
        pl.semaphore_signal(barrier, inc=1, device_id=partner, device_id_type=MESH)
    return lambda: pl.semaphore_wait(barrier, len(partners))


def remote(src, dst, send, recv, target):
    return pltpu.make_async_remote_copy(
        src_ref=src, dst_ref=dst, send_sem=send, recv_sem=recv, device_id=target, device_id_type=MESH
    )


class WeightSum:
    def __init__(self, where, nz, nh, refs):
        self.z, self.x, self.w, self.h = where
        self.nz, self.nh = nz, nh
        (self.mine, self.got1, self.mid, self.got2, self.last, self.got3, self.done) = refs[:7]
        (self.s1, self.r1, self.s2, self.r2, self.s3, self.r3, self.s4, self.r4) = refs[7:15]
        self.share = self.mine.shape[1] // NX

    @staticmethod
    def scratch(nz, nh, share, width, kind):
        dma = pltpu.SemaphoreType.DMA
        two = nz // nh
        return [
            pltpu.VMEM((nz, NX * share, width), kind),
            pltpu.VMEM((nh - 1, two, NX * share, width), kind),
            pltpu.VMEM((NX, two, PAD, width), F32),
            pltpu.VMEM((NX - 1, two, PAD, width), F32),
            pltpu.VMEM((two, PAD, width), F32),
            pltpu.VMEM((nz - 1, PAD, width), F32),
            pltpu.VMEM((PAD, width), F32),
            dma((nh - 1, two)),
            dma((nh - 1, two)),
            dma((NX - 1,)),
            dma((NX - 1,)),
            dma((two,)),
            dma((nz - 1,)),
            dma((nh - 1,)),
            dma,
        ]

    def copies1(self):
        out = []
        for d in range(1, self.nh):
            peer = lax.rem(self.h + d, self.nh)
            for i in range(self.nz // self.nh):
                e = self.nh - d - 1
                out.append(
                    remote(
                        self.mine.at[peer + i * self.nh],
                        self.got1.at[e, i],
                        self.s1.at[d - 1, i],
                        self.r1.at[e, i],
                        (self.w, peer),
                    )
                )
        return out

    def copies2(self):
        out = []
        for d in range(1, NX):
            peer = lax.rem(self.x + d, NX)
            e = NX - d - 1
            out.append(
                remote(
                    self.mid.at[peer],
                    self.got2.at[e],
                    self.s2.at[d - 1],
                    self.r2.at[e],
                    (self.z * NX + peer, self.h),
                )
            )
        return out

    def each3(self, act):
        for i in range(self.nz // self.nh):
            there = self.h + i * self.nh
            off = lax.rem(self.z - there + self.nz, self.nz)

            @pl.when(off != 0)
            def _():
                act(
                    remote(
                        self.last.at[i],
                        self.got3.at[off - 1],
                        self.s3.at[i],
                        self.r3.at[off - 1],
                        (there * NX + self.x, self.h),
                    )
                )

    def copies4(self):
        return [
            remote(
                self.done, self.done, self.s4.at[d - 1], self.r4, (self.w, lax.rem(self.h + d, self.nh))
            )
            for d in range(1, self.nh)
        ]

    def stage1(self):
        for copy in self.copies1():
            copy.start()

    def stage2(self):
        self.mid[...] = jnp.zeros_like(self.mid)
        for copy in self.copies1():
            copy.wait_recv()
        for i in range(self.nz // self.nh):
            sums = self.mine[self.h + i * self.nh].astype(F32)
            for e in range(self.nh - 1):
                sums = sums + self.got1[e, i].astype(F32)
            for peer in range(NX):
                self.mid[peer, i, : self.share] = sums[peer * self.share : (peer + 1) * self.share]
        for copy in self.copies2():
            copy.start()

    def stage3(self):
        for copy in self.copies2():
            copy.wait_recv()
        sums = self.mid[self.x]
        for e in range(NX - 1):
            sums = sums + self.got2[e]
        self.last[...] = sums
        self.each3(lambda copy: copy.start())

    def stage4(self):
        @pl.when(lax.rem(self.z, self.nh) == self.h)
        def _():
            for o in range(self.nz - 1):
                remote(
                    self.last.at[0], self.got3.at[o], self.s3.at[0], self.r3.at[o], (self.w, self.h)
                ).wait_recv()
            sums = self.last[self.z // self.nh]
            for o in range(self.nz - 1):
                sums = sums + self.got3[o]
            self.done[...] = sums
            for copy in self.copies4():
                copy.start()

    def finish(self, out):
        @pl.when(lax.rem(self.z, self.nh) != self.h)
        def _():
            self.copies4()[0].wait_recv()

        out[...] = self.done[: self.share]

    def drain(self):
        for copy in self.copies1() + self.copies2():
            copy.wait_send()
        self.each3(lambda copy: copy.wait_send())

        @pl.when(lax.rem(self.z, self.nh) == self.h)
        def _():
            for copy in self.copies4():
                copy.wait_send()


class AuthorSum:
    def __init__(self, where, nz, nh, refs):
        self.z, self.x, self.w, self.h = where
        self.nz, self.nh, self.np = nz, nh, nz // 2
        (self.mine, self.got1, self.mid, self.got2, self.cut, self.got3, self.sums4, self.rows5) = refs[:8]
        (self.s1, self.r1, self.s2, self.r2, self.s3, self.r3, self.s4, self.r4, self.s5, self.r5) = refs[8:18]

    @staticmethod
    def scratch(nz, nh, rows, width):
        dma = pltpu.SemaphoreType.DMA
        part = rows // NX
        pieces = nz // 2
        return [
            pltpu.VMEM((nh, rows, width), F32),
            pltpu.VMEM((nh - 1, rows, width), F32),
            pltpu.VMEM((NX, part, width), F32),
            pltpu.VMEM((NX - 1, part, width), F32),
            pltpu.VMEM((pieces, 8, width // 2), F32),
            pltpu.VMEM((nz - 1, 8, width // 2), F32),
            pltpu.VMEM((pieces, 8, width // 2), F32),
            pltpu.VMEM((NX, part, width), F32),
            dma((nh - 1,)),
            dma((nh - 1,)),
            dma((NX - 1,)),
            dma((NX - 1,)),
            dma((nz - 1,)),
            dma((nz - 1,)),
            dma((pieces - 1,)),
            dma((pieces - 1,)),
            dma((NX - 1,)),
            dma((NX - 1,)),
        ]

    def copies1(self):
        out = []
        for d in range(1, self.nh):
            peer = lax.rem(self.h + d, self.nh)
            e = self.nh - d - 1
            out.append(
                remote(self.mine.at[peer], self.got1.at[e], self.s1.at[d - 1], self.r1.at[e], (self.w, peer))
            )
        return out

    def copies2(self):
        out = []
        for d in range(1, NX):
            peer = lax.rem(self.x + d, NX)
            e = NX - d - 1
            to = (self.z * NX + peer, self.h)
            out.append(remote(self.mid.at[peer], self.got2.at[e], self.s2.at[d - 1], self.r2.at[e], to))
        return out

    def copies3(self):
        out = []
        for d in range(1, self.nz):
            peer = lax.rem(self.z + d, self.nz)
            e = self.nz - d - 1
            to = (peer * NX + self.x, self.h)
            out.append(
                remote(
                    self.cut.at[lax.rem(peer, self.np)], self.got3.at[e], self.s3.at[d - 1], self.r3.at[e], to
                )
            )
        return out

    def copies4(self, coming=False):
        out = []
        p = lax.rem(self.z, self.np)
        for d in range(1, self.np):
            other = lax.rem(p + d, self.np)
            to = ((self.z - p + other) * NX + self.x, self.h)
            e = d - 1 if coming else self.np - d - 1
            piece = self.sums4.at[other if coming else p]
            out.append(remote(piece, piece, self.s4.at[d - 1], self.r4.at[e], to))
        return out

    def copies5(self, coming=False):
        out = []
        for d in range(1, NX):
            peer = lax.rem(self.x + d, NX)
            e = d - 1 if coming else NX - d - 1
            rows = self.rows5.at[peer if coming else self.x]
            out.append(remote(rows, rows, self.s5.at[d - 1], self.r5.at[e], (self.z * NX + peer, self.h)))
        return out

    def stage1(self):
        for copy in self.copies1():
            copy.start()

    def stage2(self):
        for copy in self.copies1():
            copy.wait_recv()
        sums = self.mine[self.h]
        for e in range(self.nh - 1):
            sums = sums + self.got1[e]
        self.mid[...] = sums.reshape(self.mid.shape)
        for copy in self.copies2():
            copy.start()

    def stage3(self):
        for copy in self.copies2():
            copy.wait_recv()
        sums = self.mid[self.x]
        for e in range(NX - 1):
            sums = sums + self.got2[e]
        lanes = self.cut.shape[2]
        for p in range(self.np):
            g, c = p // 2, p % 2
            self.cut[p] = sums[g * 8 : (g + 1) * 8, c * lanes : (c + 1) * lanes]
        for copy in self.copies3():
            copy.start()

    def stage4(self):
        for copy in self.copies3():
            copy.wait_recv()
        p = lax.rem(self.z, self.np)
        sums = self.cut[p]
        for e in range(self.nz - 1):
            sums = sums + self.got3[e]
        self.sums4[p] = sums
        for copy in self.copies4():
            copy.start()

    def stage5(self):
        for copy in self.copies4(True):
            copy.wait_recv()
        lanes = self.cut.shape[2]
        for p in range(self.np):
            g, c = p // 2, p % 2
            self.rows5[self.x, g * 8 : (g + 1) * 8, c * lanes : (c + 1) * lanes] = self.sums4[p]
        for copy in self.copies5():
            copy.start()

    def finish(self, out):
        for copy in self.copies5(True):
            copy.wait_recv()
        out[...] = self.rows5[...].reshape(out.shape)

    def drain(self):
        for copy in self.copies1() + self.copies2() + self.copies3() + self.copies4() + self.copies5():
            copy.wait_send()


def layer_kernel(names, nz, nh, *refs):
    r = dict(zip(names, refs))
    half = nz // 2
    feat, w_cite, w_self, hot, ids, req, values, cotangent, used, target = refs[:10]
    hidden, self_out, cite_out, author_out = refs[10:14]
    own, packed, table, asks, asked, arrived = (
        r[n] for n in ("own", "packed", "table", "asks", "asked", "arrived")
    )
    spread, turned, counts, feat_t, base, total, grad, scaled = (
        r[n] for n in ("spread", "turned", "counts", "feat_t", "base", "total", "grad", "scaled")
    )
    where = place(nz)
    z, x, w, h = where
    selfs = WeightSum(where, nz, nh, [r["self%d" % i] for i in range(15)])
    cites = WeightSum(where, nz, nh, [r["cite%d" % i] for i in range(15)])
    authors = AuthorSum(where, nz, nh, [r["author%d" % i] for i in range(18)])
    blocks, size, width = own.shape
    hot_rows = hot.shape[0]
    hot_total = table.shape[0]
    per = blocks // SUBS
    to_right = (lax.rem(z + 1, nz) * NX + x, h)
    to_left = (lax.rem(z + nz - 1, nz) * NX + x, h)
    z_peers = [(lax.rem(z + d, nz) * NX + x, h) for d in range(1, nz)]
    x_peers = [(z * NX + lax.rem(x + d, NX), h) for d in range(1, NX)]
    h_peers = [(w, lax.rem(h + d, nh)) for d in range(1, nh)]
    wait_all = greet(z_peers + x_peers + h_peers)

    my_rows = pl.ds(pl.multiple_of(h * hot_rows, hot_rows), hot_rows)
    table[my_rows] = hot[...].astype(BF16)
    asks[0] = req[...]

    def spot(zoff):
        if zoff == 0:
            return 0
        return 2 * zoff if zoff < half else 2 * (nz - zoff) - 1

    def offsets(k):
        return [0] if k == 0 else [half] if k == half else [nz - k, k]

    f_right = [own] + [r["f_right%d" % k] for k in range(1, half + 1)]
    f_left = [own] + [r["f_left%d" % k] for k in range(1, half)] + [f_right[half]]
    rows_f32 = lax.broadcasted_iota(jnp.int32, (size, size), 0)

    def goes(side, k, s):
        if k > half:
            return False
        return k < half or (s < SUBS // 2) == (side == "r")

    def f_ring(side, k, s):
        part = pl.ds(s * per, per)
        bufs, to = (f_right, to_right) if side == "r" else (f_left, to_left)
        return remote(
            bufs[k - 1].at[part],
            bufs[k].at[part],
            r["fs_" + side].at[k - 1, s],
            r["fr_" + side].at[k - 1, s],
            to,
        )

    wait_all()
    for s in range(SUBS):
        rows = pl.ds(s * per * size, per * size)
        own[s * per : (s + 1) * per] = (
            jnp.dot(feat[rows], w_cite[...], preferred_element_type=F32)
            .astype(BF16)
            .reshape(per, size, width)
        )
        for side in "rl":
            if goes(side, 1, s):
                f_ring(side, 1, s).start()

    def ask_copies(coming):
        return [
            remote(
                asks.at[0],
                asks.at[d if coming else NX - d],
                r["q_send"].at[d - 1],
                r["q_recv"].at[d - 1 if coming else NX - d - 1],
                x_peers[d - 1],
            )
            for d in range(1, NX)
        ]

    def hot_copies(coming):
        out = []
        for d in range(1, nh):
            peer = lax.rem(h + d, nh) if coming else h
            rows = table.at[pl.ds(pl.multiple_of(peer * hot_rows, hot_rows), hot_rows)]
            e = d - 1 if coming else nh - d - 1
            out.append(remote(rows, rows, r["h_send"].at[d - 1], r["h_recv"].at[e], h_peers[d - 1]))
        return out

    for copy in ask_copies(False) + hot_copies(False):
        copy.start()
    for copy in ask_copies(True):
        copy.wait_recv()
    local = pltpu.make_async_copy(asks, asked, r["q_local"])
    local.start()
    local.wait()

    def owner_at(zoff, d):
        return lax.rem(z + zoff, nz) * NX + lax.rem(x + d, NX)

    def f_copy(zoff, d, coming):
        return remote(
            packed.at[d - 1, zoff],
            arrived.at[spot(zoff), d if coming else NX - d],
            r["fx_send"].at[d - 1, zoff],
            r["fx_recv"].at[d - 1 if coming else NX - d - 1, zoff],
            x_peers[d - 1],
        )

    def f_exchange(zoff, source):
        owner = owner_at(zoff, 0)
        for d in range(1, NX):
            packed[d - 1, zoff] = source[jnp.maximum(asked[d, 0, owner], 0)]
            f_copy(zoff, d, False).start()
        arrived[spot(zoff), 0] = source[jnp.maximum(asked[0, 0, owner], 0)]

    def tile_of(zoff, d):
        t = asked[0, 1, owner_at(zoff, d)]
        number = jnp.maximum(t, 0)
        return values[number].astype(F32), jnp.where(t < 0, 0, used[number]), target[number]

    def prepare(k):
        held = spread.at[k % 2]
        n = 0
        for zoff in offsets(k):
            for d in range(NX):
                m, live, block = tile_of(zoff, d)
                turned[spot(zoff), d] = jnp.where(rows_f32 < live, m, 0.0).T.astype(BF16)

                def lay(j, carry, m=m, live=live, block=block, n=n):
                    there = jnp.where(block == j, live, 0)
                    rows = pl.ds(pl.multiple_of(j * size, size), size)
                    held[rows, n * size : (n + 1) * size] = jnp.where(rows_f32 < there, m, 0.0).astype(BF16)
                    return carry

                lax.fori_loop(0, blocks, lay, 0)
                n += 1
        ones = jnp.ones((n * size, size), BF16)

        def degrees(j, carry):
            rows = pl.ds(pl.multiple_of(j * size, size), size)
            more = jnp.dot(held[rows, : n * size], ones, preferred_element_type=F32)
            total[rows, width:] = more if k == 0 else total[rows, width:] + more
            return carry

        lax.fori_loop(0, blocks, degrees, 0)

    def messages(k):
        for zoff in offsets(k):
            for d in range(1, NX):
                f_copy(zoff, d, True).wait_recv()
        first = spot(offsets(k)[0])
        count = len(offsets(k))
        span = count * NX * size

        def gather(j, carry):
            rows = pl.ds(pl.multiple_of(j * size, size), size)
            more = jnp.dot(
                spread[k % 2, rows, :span],
                arrived[first : first + count].reshape(span, width),
                preferred_element_type=F32,
            )
            total[rows, :width] = more if k == 0 else total[rows, :width] + more
            return carry

        lax.fori_loop(0, blocks, gather, 0)

    def rows_of(i):
        rows = pl.ds(i * size, size)
        names = lax.broadcasted_iota(jnp.int32, (hot_total, size), 0)
        many = jnp.zeros((hot_total, size), F32)
        for k in range(HK):
            many = many + jnp.where(ids[k : k + 1, rows] == names, 1.0, 0.0)
        many = many.astype(BF16)
        counts[:, rows] = many
        mix = lax.dot_general(many, table[...], (((0,), (0,)), ((), ())), preferred_element_type=F32)
        base[rows] = jnp.dot(feat[rows], w_self[...], preferred_element_type=F32) + mix * (1.0 / HK)
        feat_t[:, rows] = feat[rows].astype(F32).T.astype(BF16)

    f_exchange(0, own)
    prepare(0)
    prepare(1)
    for k in range(1, half + 1):
        for s in range(SUBS):
            for side in "rl":
                if goes(side, k, s):
                    f_ring(side, k, s).wait_recv()
                if goes(side, k + 1, s):
                    f_ring(side, k + 1, s).start()
        f_exchange(nz - k, f_right[k])
        if k < half:
            f_exchange(k, f_left[k])
        messages(k - 1)
        if k < half:
            prepare(k + 1)
        if k == 1:
            for copy in hot_copies(True):
                copy.wait_recv()
        for i in range(blocks):
            if i * (half - 1) // blocks == k - 1:
                rows_of(i)
    messages(half)

    def finish(j, carry):
        rows = pl.ds(pl.multiple_of(j * size, size), size)
        inv = 1.0 / jnp.maximum(total[rows, width : width + 1], 1.0)
        pre = base[rows] + total[rows, :width] * inv
        s = jax.nn.sigmoid(pre)
        hidden[rows] = (pre * s).astype(BF16)
        g = (cotangent[rows].astype(F32) * s * (1.0 + pre * (1.0 - s))).astype(BF16)
        grad[rows] = g
        scaled[j] = (g.astype(F32) * inv).astype(BF16)
        return carry

    lax.fori_loop(0, blocks, finish, 0)

    back, came, mine, far, near = (r[n] for n in ("back", "came", "mine", "far", "near"))
    b_right = [r["b_right%d" % k] for k in range(half)]
    b_left = [r["b_left%d" % k] for k in range(half)]

    def b_copy(zoff, d, coming):
        return remote(
            back.at[d - 1, zoff],
            came.at[d - 1 if coming else NX - d - 1, zoff],
            r["bx_send"].at[d - 1, zoff],
            r["bx_recv"].at[d - 1 if coming else NX - d - 1, zoff],
            x_peers[d - 1],
        )

    def b_exchange(zoff):
        for d in [*range(1, NX), 0]:
            block = target[jnp.maximum(asked[0, 1, owner_at(zoff, d)], 0)]
            value = jnp.dot(turned[spot(zoff), d], scaled[block], preferred_element_type=F32).astype(BF16)
            if d == 0:
                mine[zoff] = value
            else:
                back[d - 1, zoff] = value
                b_copy(zoff, d, False).start()

    def b_arrive(zoff):
        for d in range(1, NX):
            b_copy(zoff, d, True).wait_recv()

    step_rows = min(size, 32)

    def add_local(dst, sources, s, zoff):
        wanted = [asked[d, 0, owner_at(zoff, 0)] for d in range(NX)]

        def body(i, carry):
            rows = pl.ds(pl.multiple_of(i * step_rows, step_rows), step_rows)
            terms = [mine[zoff, rows].astype(F32)]
            for d in range(1, NX):
                terms.append(came[d - 1, zoff, rows].astype(F32))
            for j in range(s * per, (s + 1) * per):
                sums = None
                for d in range(NX):
                    term = jnp.where(wanted[d] == j, terms[d], 0.0)
                    sums = term if sums is None else sums + term
                for source in sources:
                    sums = sums + source[j, rows].astype(F32)
                dst[j, rows] = sums.astype(BF16)
            return carry

        lax.fori_loop(0, size // step_rows, body, 0)

    def b_ring(side, k, s):
        part = pl.ds(s * per, per)
        bufs, to = (b_right, to_right) if side == "r" else (b_left, to_left)
        src = far if k == half else bufs[k]
        return remote(
            src.at[part], bufs[k - 1].at[part], r["bs_" + side].at[k - 1, s], r["br_" + side].at[k - 1, s], to
        )

    group = selfs.mine.shape[1]

    def weight_product(rhs, dest):
        def body(i, carry):
            rows = pl.ds(pl.multiple_of(i * 4 * group, 4 * group), 4 * group)
            value = jnp.dot(feat_t[rows], rhs, preferred_element_type=F32)
            for q in range(4):
                dest.mine[i * 4 + q] = value[q * group : (q + 1) * group].astype(dest.mine.dtype)
            return carry

        lax.fori_loop(0, nz // 4, body, 0)

    def self_start():
        weight_product(grad[...], selfs)
        selfs.stage1()

    def author_start():
        def body(i, carry):
            rows = pl.ds(pl.multiple_of(i * hot_rows, hot_rows), hot_rows)
            authors.mine[i] = jnp.dot(counts[rows], grad[...], preferred_element_type=F32) * (1.0 / HK)
            return carry

        lax.fori_loop(0, nh, body, 0)
        authors.stage1()

    extras = [
        self_start,
        author_start,
        selfs.stage2,
        authors.stage2,
        selfs.stage3,
        authors.stage3,
        selfs.stage4,
        authors.stage4,
        authors.stage5,
        lambda: selfs.finish(self_out),
        lambda: authors.finish(author_out),
    ]
    b_exchange(half)
    for zoff in offsets(half - 1):
        b_exchange(zoff)
    for k in range(half, 0, -1):
        for zoff in offsets(k):
            b_arrive(zoff)
        for s in range(SUBS):
            for side in "rl":
                if not goes(side, k, s):
                    continue
                bufs = b_right if side == "r" else b_left
                sources = []
                if k < half and goes(side, k + 1, s):
                    b_ring(side, k + 1, s).wait_recv()
                    sources = [bufs[k]]
                add_local(far if k == half else bufs[k], sources, s, k if side == "r" else nz - k)
                b_ring(side, k, s).start()
        if k >= 2:
            for zoff in offsets(k - 2):
                b_exchange(zoff)
        first = (half - k) * len(extras) // half
        last = (half - k + 1) * len(extras) // half
        for extra in extras[first:last]:
            extra()
    b_arrive(0)
    for s in range(SUBS):
        b_ring("r", 1, s).wait_recv()
        b_ring("l", 1, s).wait_recv()
        add_local(near, [b_right[0], b_left[0]], s, 0)
    weight_product(near[...].reshape(blocks * size, width), cites)
    cites.stage1()
    for copy in ask_copies(False) + hot_copies(False):
        copy.wait_send()
    for zoff in range(nz):
        for d in range(1, NX):
            f_copy(zoff, d, False).wait_send()
            b_copy(zoff, d, False).wait_send()
    for k in range(1, half + 1):
        for s in range(SUBS):
            for side in "rl":
                if goes(side, k, s):
                    f_ring(side, k, s).wait_send()
                    b_ring(side, k, s).wait_send()
    selfs.drain()
    authors.drain()
    cites.stage2()
    cites.stage3()
    cites.stage4()
    cites.finish(cite_out)
    cites.drain()


def layer(nz, nh, feat, w_cite, w_self, hot, ids, req, values, cotangent, used, target):
    half = nz // 2
    rows, din = feat.shape
    width = w_self.shape[1]
    size = values.shape[1]
    blocks = rows // size
    hot_total = hot.shape[0] * nh
    share = din // (nz * NX)
    vmem = pl.BlockSpec(memory_space=pltpu.VMEM)
    smem = pl.BlockSpec(memory_space=pltpu.SMEM)
    dma = pltpu.SemaphoreType.DMA
    chunk = pltpu.VMEM((blocks, size, width), BF16)
    column = pltpu.VMEM((NX - 1, nz, size, width), BF16)
    scratch = {
        "own": chunk,
        "packed": column,
        "table": pltpu.VMEM((hot_total, width), BF16),
        "asks": pltpu.VMEM((NX,) + req.shape, jnp.int32),
        "asked": pltpu.SMEM((NX,) + req.shape, jnp.int32),
        "arrived": pltpu.VMEM((nz, NX, size, width), BF16),
        "spread": pltpu.VMEM((2, rows, 2 * NX * size), BF16),
        "turned": pltpu.VMEM((nz, NX, size, size), BF16),
        "counts": pltpu.VMEM((hot_total, rows), BF16),
        "feat_t": pltpu.VMEM((din, rows), BF16),
        "base": pltpu.VMEM((rows, width), F32),
        "total": pltpu.VMEM((rows, width + size), F32),
        "grad": pltpu.VMEM((rows, width), BF16),
        "scaled": chunk,
        "back": column,
        "came": column,
        "mine": pltpu.VMEM((nz, size, width), BF16),
        "far": chunk,
        "near": chunk,
        "h_send": dma((nh - 1,)),
        "h_recv": dma((nh - 1,)),
        "q_send": dma((NX - 1,)),
        "q_recv": dma((NX - 1,)),
        "q_local": dma,
    }
    for k in range(1, half + 1):
        scratch["f_right%d" % k] = chunk
    for k in range(1, half):
        scratch["f_left%d" % k] = chunk
    for k in range(half):
        scratch["b_right%d" % k] = chunk
        scratch["b_left%d" % k] = chunk
    for name in ("fs_r", "fr_r", "fs_l", "fr_l", "bs_r", "br_r", "bs_l", "br_l"):
        scratch[name] = dma((half, SUBS))
    for name in ("fx_send", "fx_recv", "bx_send", "bx_recv"):
        scratch[name] = dma((NX - 1, nz))
    for name, parts in (
        ("self", WeightSum.scratch(nz, nh, share, width, F32)),
        ("cite", WeightSum.scratch(nz, nh, share, width, BF16)),
        ("author", AuthorSum.scratch(nz, nh, hot.shape[0], width)),
    ):
        for i, part in enumerate(parts):
            scratch[name + str(i)] = part
    names = ["in%d" % i for i in range(10)] + ["out%d" % i for i in range(4)] + list(scratch)
    return pl.pallas_call(
        functools.partial(layer_kernel, names, nz, nh),
        out_shape=(
            jax.ShapeDtypeStruct((rows, width), BF16),
            jax.ShapeDtypeStruct((share, width), F32),
            jax.ShapeDtypeStruct((share, width), F32),
            jax.ShapeDtypeStruct(hot.shape, F32),
        ),
        in_specs=[vmem] * 8 + [smem] * 2,
        out_specs=(vmem,) * 4,
        scratch_shapes=list(scratch.values()),
        compiler_params=pltpu.CompilerParams(
            collective_id=1, has_side_effects=True, vmem_limit_bytes=VMEM_LIMIT
        ),
    )(feat, w_cite, w_self, hot, ids, req, values, cotangent, used, target)


def hand_over_kernel(*refs):
    half = len(refs) // 2
    for src, dst in zip(refs[:half], refs[half:]):
        dst[...] = src[...]


def hand_over(arrays):
    vmem = pl.BlockSpec(memory_space=pltpu.VMEM)
    return pl.pallas_call(
        hand_over_kernel,
        out_shape=tuple(jax.ShapeDtypeStruct(a.shape, a.dtype) for a in arrays),
        in_specs=[vmem] * len(arrays),
        out_specs=(vmem,) * len(arrays),
    )(*arrays)


def on_device(
    paper_features,
    self_weight,
    cite_weight,
    hot_embed,
    hot_ids,
    tile_values,
    tile_rows,
    tile_target_block,
    tile_block,
    tile_owner,
    cotangent,
):
    wide = lax.axis_size("wide")
    nh = lax.axis_size("hot")
    nz = wide // NX
    tiles = tile_values.shape[0]
    shape = (8, tiles, max(128, wide))
    what = jnp.where(
        lax.broadcasted_iota(jnp.int32, shape, 0) == 0,
        tile_block[None, :, None],
        lax.broadcasted_iota(jnp.int32, shape, 1),
    )
    owned = tile_owner[None, :, None] == lax.broadcasted_iota(jnp.int32, shape, 2)
    req = jnp.max(jnp.where(owned, what, -1), axis=1)
    return hand_over(
        layer(
            nz,
            nh,
            paper_features,
            cite_weight,
            self_weight,
            hot_embed,
            hot_ids.T,
            req,
            tile_values,
            cotangent,
            tile_rows,
            tile_target_block,
        )
    )


def solution(mesh):
    return jax.shard_map(
        on_device,
        mesh=mesh,
        in_specs=(
            P(("wide", "hot"), None),
            P(),
            P(),
            P("hot", None),
            P(("wide", "hot"), None),
            P(("wide", "hot"), None, None),
            P(("wide", "hot")),
            P(("wide", "hot")),
            P(("wide", "hot")),
            P(("wide", "hot")),
            P(("wide", "hot"), None),
        ),
        out_specs=(P(("wide", "hot"), None), P("wide", None), P("wide", None), P("hot", None)),
        check_vma=False,
    )
```

time: 269 us -> 240 us (0.89)
  Pallas kernels: 259 us -> 237 us
  local copies, waits for them, and re-layouts: 6.56 us -> 0 us
    pallas_call x3 -> x2, Pallas kernels: 259 us -> 237 us  [the longest x1 236 us: layer(): pl.pallas_call(functools.partial(layer_kernel, names, nz, nh), out_shape=...]
    unnamed x4 -> x0, local copies, waits for them, and re-layouts: 5.97 us -> none
where the time goes in v2:
time: 240 us
  Pallas kernels  237 us (99%)
    pallas_call x1, Pallas kernels, layer(): pl.pallas_call(functools.partial(layer_kernel, names, nz, nh), out_shape=...  236 us

profile of v2, /device:TPU:17, one launch (start us, length us, event | category | flops | bytes accessed | tf_op | source)
XLA Modules:
  0.0 239.5 jit_solution(12675403314896635401)
XLA Ops:
  0.6 1.4 select_reduce_fusion.refs_5_
  2.0 235.5 %shard_map.138 = (bf16[1024,256]{1,0:T(8,128)(2,1)}, f32[12,256]{1,0:T(8,128)}, f32[12,256]{1,0:T(8,128)}, f32[128,256]{1,0:T(8,128)}) custom-call(bf16[1024,768]{1,0:T(8,128)(2,1)} %refs_0_.1, bf16[768,256]{1,0:T(8,128)(2,1)} %refs_1_.1, bf16[768,256]{1,0:T(8,128)(2,1)} %refs_2_.1, f32[128,256]{1,0:T(8,128)} %refs_3_.1, s32[8,1024]{1,0:T(8,128)} %bitcast.1, ...), custom_call_target="tpu_custom_call" | custom-call | tf_op jit(solution)/shard_map/pallas_call | solution.py:752
  237.5 2.0 shard_map.139
  (1 shorter events, 0.0 us)

commit v3 on v2

--- a/solution.py
+++ b/solution.py
@@ -9,7 +9,7 @@
 
 HK = 8
 NX = 4
-SUBS = 4
+SUBS = 8
 PAD = 16
 MESH = pl.DeviceIdType.MESH
 F32 = jnp.float32
@@ -41,7 +41,7 @@
         self.z, self.x, self.w, self.h = where
         self.nz, self.nh = nz, nh
         (self.mine, self.got1, self.mid, self.got2, self.last, self.got3, self.done) = refs[:7]
-        (self.s1, self.r1, self.s2, self.r2, self.s3, self.r3, self.s4, self.r4) = refs[7:15]
+        (self.wide, self.s1, self.r1, self.s2, self.r2, self.s3, self.r3, self.s4, self.r4) = refs[7:16]
         self.share = self.mine.shape[1] // NX
 
     @staticmethod
@@ -51,11 +51,12 @@
         return [
             pltpu.VMEM((nz, NX * share, width), kind),
             pltpu.VMEM((nh - 1, two, NX * share, width), kind),
+            pltpu.VMEM((NX, two, PAD, width), BF16),
+            pltpu.VMEM((NX - 1, two, PAD, width), BF16),
+            pltpu.VMEM((two, PAD, width), BF16),
+            pltpu.VMEM((nz - 1, PAD, width), BF16),
+            pltpu.VMEM((PAD, width), F32),
             pltpu.VMEM((NX, two, PAD, width), F32),
-            pltpu.VMEM((NX - 1, two, PAD, width), F32),
-            pltpu.VMEM((two, PAD, width), F32),
-            pltpu.VMEM((nz - 1, PAD, width), F32),
-            pltpu.VMEM((PAD, width), F32),
             dma((nh - 1, two)),
             dma((nh - 1, two)),
             dma((NX - 1,)),
@@ -129,7 +130,7 @@
             copy.start()
 
     def stage2(self):
-        self.mid[...] = jnp.zeros_like(self.mid)
+        self.wide[...] = jnp.zeros_like(self.wide)
         for copy in self.copies1():
             copy.wait_recv()
         for i in range(self.nz // self.nh):
@@ -137,17 +138,19 @@
             for e in range(self.nh - 1):
                 sums = sums + self.got1[e, i].astype(F32)
             for peer in range(NX):
-                self.mid[peer, i, : self.share] = sums[peer * self.share : (peer + 1) * self.share]
+                self.wide[peer, i, : self.share] = sums[peer * self.share : (peer + 1) * self.share]
+        self.mid[...] = self.wide[...].astype(BF16)
         for copy in self.copies2():
             copy.start()
 
     def stage3(self):
         for copy in self.copies2():
             copy.wait_recv()
-        sums = self.mid[self.x]
+        sums = self.wide[self.x]
         for e in range(NX - 1):
-            sums = sums + self.got2[e]
-        self.last[...] = sums
+            sums = sums + self.got2[e].astype(F32)
+        self.wide[self.x] = sums
+        self.last[...] = sums.astype(BF16)
         self.each3(lambda copy: copy.start())
 
     def stage4(self):
@@ -157,9 +160,9 @@
                 remote(
                     self.last.at[0], self.got3.at[o], self.s3.at[0], self.r3.at[o], (self.w, self.h)
                 ).wait_recv()
-            sums = self.last[self.z // self.nh]
+            sums = self.wide[self.x, self.z // self.nh]
             for o in range(self.nz - 1):
-                sums = sums + self.got3[o]
+                sums = sums + self.got3[o].astype(F32)
             self.done[...] = sums
             for copy in self.copies4():
                 copy.start()
@@ -338,8 +341,8 @@
     )
     where = place(nz)
     z, x, w, h = where
-    selfs = WeightSum(where, nz, nh, [r["self%d" % i] for i in range(15)])
-    cites = WeightSum(where, nz, nh, [r["cite%d" % i] for i in range(15)])
+    selfs = WeightSum(where, nz, nh, [r["self%d" % i] for i in range(16)])
+    cites = WeightSum(where, nz, nh, [r["cite%d" % i] for i in range(16)])
     authors = AuthorSum(where, nz, nh, [r["author%d" % i] for i in range(18)])
     blocks, size, width = own.shape
     hot_rows = hot.shape[0]
@@ -384,14 +387,14 @@
             to,
         )
 
+    def project(j, carry):
+        rows = pl.ds(pl.multiple_of(j * size, size), size)
+        own[j] = jnp.dot(feat[rows], w_cite[...], preferred_element_type=F32).astype(BF16)
+        return carry
+
+    lax.fori_loop(0, blocks, project, 0)
     wait_all()
     for s in range(SUBS):
-        rows = pl.ds(s * per * size, per * size)
-        own[s * per : (s + 1) * per] = (
-            jnp.dot(feat[rows], w_cite[...], preferred_element_type=F32)
-            .astype(BF16)
-            .reshape(per, size, width)
-        )
         for side in "rl":
             if goes(side, 1, s):
                 f_ring(side, 1, s).start()
@@ -449,31 +452,39 @@
         number = jnp.maximum(t, 0)
         return values[number].astype(F32), jnp.where(t < 0, 0, used[number]), target[number]
 
-    def prepare(k):
+    def lay_out(k, zoff, d):
         held = spread.at[k % 2]
-        n = 0
-        for zoff in offsets(k):
-            for d in range(NX):
-                m, live, block = tile_of(zoff, d)
-                turned[spot(zoff), d] = jnp.where(rows_f32 < live, m, 0.0).T.astype(BF16)
-
-                def lay(j, carry, m=m, live=live, block=block, n=n):
-                    there = jnp.where(block == j, live, 0)
-                    rows = pl.ds(pl.multiple_of(j * size, size), size)
-                    held[rows, n * size : (n + 1) * size] = jnp.where(rows_f32 < there, m, 0.0).astype(BF16)
-                    return carry
-
-                lax.fori_loop(0, blocks, lay, 0)
-                n += 1
-        ones = jnp.ones((n * size, size), BF16)
-
-        def degrees(j, carry):
+        n = offsets(k).index(zoff) * NX + d
+        m, live, block = tile_of(zoff, d)
+        turned[spot(zoff), d] = jnp.where(rows_f32 < live, m, 0.0).T.astype(BF16)
+
+        def lay(j, carry):
+            there = jnp.where(block == j, live, 0)
             rows = pl.ds(pl.multiple_of(j * size, size), size)
-            more = jnp.dot(held[rows, : n * size], ones, preferred_element_type=F32)
+            held[rows, n * size : (n + 1) * size] = jnp.where(rows_f32 < there, m, 0.0).astype(BF16)
+            return carry
+
+        lax.fori_loop(0, blocks, lay, 0)
+
+    def degrees(k):
+        span = len(offsets(k)) * NX * size
+        ones = jnp.ones((span, size), BF16)
+
+        def body(j, carry):
+            rows = pl.ds(pl.multiple_of(j * size, size), size)
+            more = jnp.dot(spread[k % 2, rows, :span], ones, preferred_element_type=F32)
             total[rows, width:] = more if k == 0 else total[rows, width:] + more
             return carry
 
-        lax.fori_loop(0, blocks, degrees, 0)
+        lax.fori_loop(0, blocks, body, 0)
+
+    def prepare(k):
+        parts = [functools.partial(lay_out, k, zoff, d) for zoff in offsets(k) for d in range(NX)]
+        return parts + [functools.partial(degrees, k)]
+
+    def share_out(work, s):
+        for item in work[s * len(work) // SUBS : (s + 1) * len(work) // SUBS]:
+            item()
 
     def messages(k):
         for zoff in offsets(k):
@@ -495,40 +506,67 @@
 
         lax.fori_loop(0, blocks, gather, 0)
 
-    def rows_of(i):
+    def count(i):
         rows = pl.ds(i * size, size)
-        names = lax.broadcasted_iota(jnp.int32, (hot_total, size), 0)
-        many = jnp.zeros((hot_total, size), F32)
-        for k in range(HK):
-            many = many + jnp.where(ids[k : k + 1, rows] == names, 1.0, 0.0)
-        many = many.astype(BF16)
-        counts[:, rows] = many
-        mix = lax.dot_general(many, table[...], (((0,), (0,)), ((), ())), preferred_element_type=F32)
+
+        def body(a, carry):
+            there = pl.ds(pl.multiple_of(a * hot_rows, hot_rows), hot_rows)
+            names = lax.broadcasted_iota(jnp.int32, (hot_rows, size), 0) + a * hot_rows
+            many = jnp.zeros((hot_rows, size), F32)
+            for k in range(HK):
+                many = many + jnp.where(ids[k : k + 1, rows] == names, 1.0, 0.0)
+            counts[there, rows] = many.astype(BF16)
+            return carry
+
+        lax.fori_loop(0, nh, body, 0)
+
+    def start_rows(i):
+        rows = pl.ds(i * size, size)
+        mix = lax.dot_general(
+            counts[:, rows], table[...], (((0,), (0,)), ((), ())), preferred_element_type=F32
+        )
         base[rows] = jnp.dot(feat[rows], w_self[...], preferred_element_type=F32) + mix * (1.0 / HK)
+
+    def turn(i):
+        rows = pl.ds(i * size, size)
         feat_t[:, rows] = feat[rows].astype(F32).T.astype(BF16)
 
+    def f_done(k):
+        for s in range(SUBS):
+            for side in "rl":
+                if k >= 1 and goes(side, k, s):
+                    f_ring(side, k, s).wait_send()
+        for zoff in offsets(k):
+            for d in range(1, NX):
+                f_copy(zoff, d, False).wait_send()
+
     f_exchange(0, own)
-    prepare(0)
-    prepare(1)
+    for item in prepare(0) + prepare(1):
+        item()
     for k in range(1, half + 1):
+        work = []
+        for i in range(blocks):
+            if i * (half - 1) // blocks == k - 1:
+                work += [functools.partial(part, i) for part in (turn, count, start_rows)]
+        work.append(functools.partial(messages, k - 1))
+        if k < half:
+            work += prepare(k + 1)
+        if k >= 2:
+            work.append(functools.partial(f_done, k - 2))
+        if k == 1:
+            for copy in hot_copies(True):
+                copy.wait_recv()
         for s in range(SUBS):
             for side in "rl":
                 if goes(side, k, s):
                     f_ring(side, k, s).wait_recv()
                 if goes(side, k + 1, s):
                     f_ring(side, k + 1, s).start()
-        f_exchange(nz - k, f_right[k])
-        if k < half:
-            f_exchange(k, f_left[k])
-        messages(k - 1)
-        if k < half:
-            prepare(k + 1)
-        if k == 1:
-            for copy in hot_copies(True):
-                copy.wait_recv()
-        for i in range(blocks):
-            if i * (half - 1) // blocks == k - 1:
-                rows_of(i)
+            if s == SUBS - 1:
+                f_exchange(nz - k, f_right[k])
+                if k < half:
+                    f_exchange(k, f_left[k])
+            share_out(work, s)
     messages(half)
 
     def finish(j, carry):
@@ -557,15 +595,26 @@
             x_peers[d - 1],
         )
 
-    def b_exchange(zoff):
-        for d in [*range(1, NX), 0]:
-            block = target[jnp.maximum(asked[0, 1, owner_at(zoff, d)], 0)]
-            value = jnp.dot(turned[spot(zoff), d], scaled[block], preferred_element_type=F32).astype(BF16)
-            if d == 0:
-                mine[zoff] = value
-            else:
-                back[d - 1, zoff] = value
-                b_copy(zoff, d, False).start()
+    def b_make(zoff, d):
+        block = target[jnp.maximum(asked[0, 1, owner_at(zoff, d)], 0)]
+        value = jnp.dot(turned[spot(zoff), d], scaled[block], preferred_element_type=F32).astype(BF16)
+        if d == 0:
+            mine[zoff] = value
+        else:
+            back[d - 1, zoff] = value
+            b_copy(zoff, d, False).start()
+
+    def b_exchange(k):
+        return [functools.partial(b_make, zoff, d) for d in [*range(1, NX), 0] for zoff in offsets(k)]
+
+    def b_done(k):
+        for s in range(SUBS):
+            for side in "rl":
+                if k >= 1 and goes(side, k, s):
+                    b_ring(side, k, s).wait_send()
+        for zoff in offsets(k):
+            for d in range(1, NX):
+                b_copy(zoff, d, False).wait_send()
 
     def b_arrive(zoff):
         for d in range(1, NX):
@@ -627,22 +676,25 @@
         authors.stage1()
 
     extras = [
-        self_start,
-        author_start,
-        selfs.stage2,
-        authors.stage2,
-        selfs.stage3,
-        authors.stage3,
-        selfs.stage4,
-        authors.stage4,
-        authors.stage5,
-        lambda: selfs.finish(self_out),
-        lambda: authors.finish(author_out),
+        [self_start],
+        [author_start],
+        [selfs.stage2],
+        [authors.stage2],
+        [selfs.stage3, authors.stage3],
+        [selfs.stage4],
+        [authors.stage4],
+        [authors.stage5],
     ]
-    b_exchange(half)
-    for zoff in offsets(half - 1):
-        b_exchange(zoff)
+    for item in b_exchange(half) + b_exchange(half - 1):
+        item()
     for k in range(half, 0, -1):
+        work = b_exchange(k - 2) if k >= 2 else []
+        for group_of in extras[(half - k) * 8 // half : (half - k + 1) * 8 // half]:
+            work += group_of
+        if k == half:
+            work += [functools.partial(f_done, half - 1), functools.partial(f_done, half)]
+        if k + 2 <= half:
+            work.append(functools.partial(b_done, k + 2))
         for zoff in offsets(k):
             b_arrive(zoff)
         for s in range(SUBS):
@@ -656,13 +708,7 @@
                     sources = [bufs[k]]
                 add_local(far if k == half else bufs[k], sources, s, k if side == "r" else nz - k)
                 b_ring(side, k, s).start()
-        if k >= 2:
-            for zoff in offsets(k - 2):
-                b_exchange(zoff)
-        first = (half - k) * len(extras) // half
-        last = (half - k + 1) * len(extras) // half
-        for extra in extras[first:last]:
-            extra()
+            share_out(work, s)
     b_arrive(0)
     for s in range(SUBS):
         b_ring("r", 1, s).wait_recv()
@@ -670,22 +716,16 @@
         add_local(near, [b_right[0], b_left[0]], s, 0)
     weight_product(near[...].reshape(blocks * size, width), cites)
     cites.stage1()
+    selfs.finish(self_out)
+    authors.finish(author_out)
     for copy in ask_copies(False) + hot_copies(False):
         copy.wait_send()
-    for zoff in range(nz):
-        for d in range(1, NX):
-            f_copy(zoff, d, False).wait_send()
-            b_copy(zoff, d, False).wait_send()
-    for k in range(1, half + 1):
-        for s in range(SUBS):
-            for side in "rl":
-                if goes(side, k, s):
-                    f_ring(side, k, s).wait_send()
-                    b_ring(side, k, s).wait_send()
+    for k in (2, 1, 0):
+        b_done(k)
+    cites.stage2()
     selfs.drain()
+    cites.stage3()
     authors.drain()
-    cites.stage2()
-    cites.stage3()
     cites.stage4()
     cites.finish(cite_out)
     cites.drain()

time: 240 us -> 244 us (1.017)
  Pallas kernels: 237 us -> 241 us
    pallas_call x1, Pallas kernels: 236 us -> 240 us  [layer(): pl.pallas_call(functools.partial(layer_kernel, names, nz, nh), out_shape=...]
where the time goes in v3:
time: 244 us; the launch traced here: 243 us
  Pallas kernels  241 us (99%)
    pallas_call x1, Pallas kernels, layer(): pl.pallas_call(functools.partial(layer_kernel, names, nz, nh), out_shape=...  240 us

profile of v3, /device:TPU:17, one launch (start us, length us, event | category | flops | bytes accessed | tf_op | source)
XLA Modules:
  0.0 243.5 jit_solution(3540294901031271071)
XLA Ops:
  0.6 1.4 select_reduce_fusion.refs_5_
  2.0 239.5 %shard_map.138 = (bf16[1024,256]{1,0:T(8,128)(2,1)}, f32[12,256]{1,0:T(8,128)}, f32[12,256]{1,0:T(8,128)}, f32[128,256]{1,0:T(8,128)}) custom-call(bf16[1024,768]{1,0:T(8,128)(2,1)} %refs_0_.1, bf16[768,256]{1,0:T(8,128)(2,1)} %refs_1_.1, bf16[768,256]{1,0:T(8,128)(2,1)} %refs_2_.1, f32[128,256]{1,0:T(8,128)} %refs_3_.1, s32[8,1024]{1,0:T(8,128)} %bitcast.1, ...), custom_call_target="tpu_custom_call" | custom-call | tf_op jit(solution)/shard_map/pallas_call | solution.py:792
  241.5 2.0 shard_map.139
  (1 shorter events, 0.0 us)

commit v4 on v3

--- a/solution.py
+++ b/solution.py
@@ -9,7 +9,7 @@
 
 HK = 8
 NX = 4
-SUBS = 8
+SUBS = 4
 PAD = 16
 MESH = pl.DeviceIdType.MESH
 F32 = jnp.float32
@@ -339,6 +339,7 @@
     spread, turned, counts, feat_t, base, total, grad, scaled = (
         r[n] for n in ("spread", "turned", "counts", "feat_t", "base", "total", "grad", "scaled")
     )
+    degree, inverse = r["degree"], r["inverse"]
     where = place(nz)
     z, x, w, h = where
     selfs = WeightSum(where, nz, nh, [r["self%d" % i] for i in range(16)])
@@ -444,6 +445,7 @@
         owner = owner_at(zoff, 0)
         for d in range(1, NX):
             packed[d - 1, zoff] = source[jnp.maximum(asked[d, 0, owner], 0)]
+        for d in range(1, NX):
             f_copy(zoff, d, False).start()
         arrived[spot(zoff), 0] = source[jnp.maximum(asked[0, 0, owner], 0)]
 
@@ -461,26 +463,24 @@
         def lay(j, carry):
             there = jnp.where(block == j, live, 0)
             rows = pl.ds(pl.multiple_of(j * size, size), size)
-            held[rows, n * size : (n + 1) * size] = jnp.where(rows_f32 < there, m, 0.0).astype(BF16)
+            laid = jnp.where(rows_f32 < there, m, 0.0)
+            held[rows, n * size : (n + 1) * size] = laid.astype(BF16)
+            degree[rows] = laid if k == 0 and n == 0 else degree[rows] + laid
             return carry
 
         lax.fori_loop(0, blocks, lay, 0)
 
-    def degrees(k):
-        span = len(offsets(k)) * NX * size
-        ones = jnp.ones((span, size), BF16)
-
+    def invert():
         def body(j, carry):
             rows = pl.ds(pl.multiple_of(j * size, size), size)
-            more = jnp.dot(spread[k % 2, rows, :span], ones, preferred_element_type=F32)
-            total[rows, width:] = more if k == 0 else total[rows, width:] + more
+            sums = jnp.sum(degree[rows], axis=1, keepdims=True)
+            inverse[rows] = jnp.broadcast_to(1.0 / jnp.maximum(sums, 1.0), (size, width))
             return carry
 
         lax.fori_loop(0, blocks, body, 0)
 
     def prepare(k):
-        parts = [functools.partial(lay_out, k, zoff, d) for zoff in offsets(k) for d in range(NX)]
-        return parts + [functools.partial(degrees, k)]
+        return [functools.partial(lay_out, k, zoff, d) for zoff in offsets(k) for d in range(NX)]
 
     def share_out(work, s):
         for item in work[s * len(work) // SUBS : (s + 1) * len(work) // SUBS]:
@@ -494,17 +494,19 @@
         count = len(offsets(k))
         span = count * NX * size
 
+        step = blocks * size // 2
+
         def gather(j, carry):
-            rows = pl.ds(pl.multiple_of(j * size, size), size)
+            rows = pl.ds(pl.multiple_of(j * step, step), step)
             more = jnp.dot(
                 spread[k % 2, rows, :span],
                 arrived[first : first + count].reshape(span, width),
                 preferred_element_type=F32,
             )
-            total[rows, :width] = more if k == 0 else total[rows, :width] + more
+            total[rows] = more if k == 0 else total[rows] + more
             return carry
 
-        lax.fori_loop(0, blocks, gather, 0)
+        lax.fori_loop(0, 2, gather, 0)
 
     def count(i):
         rows = pl.ds(i * size, size)
@@ -551,6 +553,8 @@
         work.append(functools.partial(messages, k - 1))
         if k < half:
             work += prepare(k + 1)
+        else:
+            work.append(invert)
         if k >= 2:
             work.append(functools.partial(f_done, k - 2))
         if k == 1:
@@ -571,8 +575,8 @@
 
     def finish(j, carry):
         rows = pl.ds(pl.multiple_of(j * size, size), size)
-        inv = 1.0 / jnp.maximum(total[rows, width : width + 1], 1.0)
-        pre = base[rows] + total[rows, :width] * inv
+        inv = inverse[rows]
+        pre = base[rows] + total[rows] * inv
         s = jax.nn.sigmoid(pre)
         hidden[rows] = (pre * s).astype(BF16)
         g = (cotangent[rows].astype(F32) * s * (1.0 + pre * (1.0 - s))).astype(BF16)
@@ -595,17 +599,19 @@
             x_peers[d - 1],
         )
 
-    def b_make(zoff, d):
-        block = target[jnp.maximum(asked[0, 1, owner_at(zoff, d)], 0)]
-        value = jnp.dot(turned[spot(zoff), d], scaled[block], preferred_element_type=F32).astype(BF16)
-        if d == 0:
-            mine[zoff] = value
-        else:
-            back[d - 1, zoff] = value
+    def b_make(zoff):
+        made = []
+        for d in range(NX):
+            block = target[jnp.maximum(asked[0, 1, owner_at(zoff, d)], 0)]
+            made.append(jnp.dot(turned[spot(zoff), d], scaled[block], preferred_element_type=F32).astype(BF16))
+        for d in range(1, NX):
+            back[d - 1, zoff] = made[d]
+        mine[zoff] = made[0]
+        for d in range(1, NX):
             b_copy(zoff, d, False).start()
 
     def b_exchange(k):
-        return [functools.partial(b_make, zoff, d) for d in [*range(1, NX), 0] for zoff in offsets(k)]
+        return [functools.partial(b_make, zoff) for zoff in offsets(k)]
 
     def b_done(k):
         for s in range(SUBS):
@@ -620,24 +626,22 @@
         for d in range(1, NX):
             b_copy(zoff, d, True).wait_recv()
 
-    step_rows = min(size, 32)
+    step_rows = min(size, 64)
 
     def add_local(dst, sources, s, zoff):
         wanted = [asked[d, 0, owner_at(zoff, 0)] for d in range(NX)]
 
         def body(i, carry):
             rows = pl.ds(pl.multiple_of(i * step_rows, step_rows), step_rows)
-            terms = [mine[zoff, rows].astype(F32)]
-            for d in range(1, NX):
-                terms.append(came[d - 1, zoff, rows].astype(F32))
+            terms = [mine[zoff, rows]] + [came[d - 1, zoff, rows] for d in range(1, NX)]
             for j in range(s * per, (s + 1) * per):
                 sums = None
                 for d in range(NX):
-                    term = jnp.where(wanted[d] == j, terms[d], 0.0)
+                    term = jnp.where(wanted[d] == j, terms[d], jnp.zeros_like(terms[d]))
                     sums = term if sums is None else sums + term
                 for source in sources:
-                    sums = sums + source[j, rows].astype(F32)
-                dst[j, rows] = sums.astype(BF16)
+                    sums = sums + source[j, rows]
+                dst[j, rows] = sums
             return carry
 
         lax.fori_loop(0, size // step_rows, body, 0)
@@ -653,14 +657,16 @@
     group = selfs.mine.shape[1]
 
     def weight_product(rhs, dest):
+        many = nz // 2
+
         def body(i, carry):
-            rows = pl.ds(pl.multiple_of(i * 4 * group, 4 * group), 4 * group)
+            rows = pl.ds(pl.multiple_of(i * many * group, many * group), many * group)
             value = jnp.dot(feat_t[rows], rhs, preferred_element_type=F32)
-            for q in range(4):
-                dest.mine[i * 4 + q] = value[q * group : (q + 1) * group].astype(dest.mine.dtype)
+            for q in range(many):
+                dest.mine[i * many + q] = value[q * group : (q + 1) * group].astype(dest.mine.dtype)
             return carry
 
-        lax.fori_loop(0, nz // 4, body, 0)
+        lax.fori_loop(0, 2, body, 0)
 
     def self_start():
         weight_product(grad[...], selfs)
@@ -668,11 +674,13 @@
 
     def author_start():
         def body(i, carry):
-            rows = pl.ds(pl.multiple_of(i * hot_rows, hot_rows), hot_rows)
-            authors.mine[i] = jnp.dot(counts[rows], grad[...], preferred_element_type=F32) * (1.0 / HK)
+            rows = pl.ds(pl.multiple_of(i * hot_total // 2, hot_total // 2), hot_total // 2)
+            value = jnp.dot(counts[rows], grad[...], preferred_element_type=F32) * (1.0 / HK)
+            for q in range(nh // 2):
+                authors.mine[i * (nh // 2) + q] = value[q * hot_rows : (q + 1) * hot_rows]
             return carry
 
-        lax.fori_loop(0, nh, body, 0)
+        lax.fori_loop(0, 2, body, 0)
         authors.stage1()
 
     extras = [
@@ -756,7 +764,9 @@
         "counts": pltpu.VMEM((hot_total, rows), BF16),
         "feat_t": pltpu.VMEM((din, rows), BF16),
         "base": pltpu.VMEM((rows, width), F32),
-        "total": pltpu.VMEM((rows, width + size), F32),
+        "total": pltpu.VMEM((rows, width), F32),
+        "degree": pltpu.VMEM((rows, size), F32),
+        "inverse": pltpu.VMEM((rows, width), F32),
         "grad": pltpu.VMEM((rows, width), BF16),
         "scaled": chunk,
         "back": column,

time: 244 us -> 238 us (0.975)
  Pallas kernels: 241 us -> 235 us
    pallas_call x1, Pallas kernels: 240 us -> 234 us  [layer(): pl.pallas_call(functools.partial(layer_kernel, names, nz, nh), out_shape=...]
where the time goes in v4:
time: 238 us
  Pallas kernels  235 us (99%)
    pallas_call x1, Pallas kernels, layer(): pl.pallas_call(functools.partial(layer_kernel, names, nz, nh), out_shape=...  234 us

profile of v4, /device:TPU:17, one launch (start us, length us, event | category | flops | bytes accessed | tf_op | source)
XLA Modules:
  0.0 237.5 jit_solution(17368221628111424620)
XLA Ops:
  0.6 1.4 select_reduce_fusion.refs_5_
  2.0 233.5 %shard_map.138 = (bf16[1024,256]{1,0:T(8,128)(2,1)}, f32[12,256]{1,0:T(8,128)}, f32[12,256]{1,0:T(8,128)}, f32[128,256]{1,0:T(8,128)}) custom-call(bf16[1024,768]{1,0:T(8,128)(2,1)} %refs_0_.1, bf16[768,256]{1,0:T(8,128)(2,1)} %refs_1_.1, bf16[768,256]{1,0:T(8,128)(2,1)} %refs_2_.1, f32[128,256]{1,0:T(8,128)} %refs_3_.1, s32[8,1024]{1,0:T(8,128)} %bitcast.1, ...), custom_call_target="tpu_custom_call" | custom-call | tf_op jit(solution)/shard_map/pallas_call | solution.py:802
  235.5 2.0 shard_map.139
  (1 shorter events, 0.0 us)

commit v5 on v4

--- a/solution.py
+++ b/solution.py
@@ -368,18 +368,21 @@
     def offsets(k):
         return [0] if k == 0 else [half] if k == half else [nz - k, k]
 
-    f_right = [own] + [r["f_right%d" % k] for k in range(1, half + 1)]
-    f_left = [own] + [r["f_left%d" % k] for k in range(1, half)] + [f_right[half]]
+    last, few = half - 2, NX // 2
+    f_right = [own] + [r["f_right%d" % k] for k in range(1, last + 1)]
+    f_left = [own] + [r["f_left%d" % k] for k in range(1, last + 1)]
     rows_f32 = lax.broadcasted_iota(jnp.int32, (size, size), 0)
+    far_devices = {"r": list(range(few)), "l": list(range(few, NX))}
+    ahead = {"r": (0, 2), "l": (1, 3)}
+    behind = {"r": (1, 3), "l": (0, 2)}
+    side_to = {"r": to_right, "l": to_left}
 
     def goes(side, k, s):
-        if k > half:
-            return False
-        return k < half or (s < SUBS // 2) == (side == "r")
+        return k <= last
 
     def f_ring(side, k, s):
         part = pl.ds(s * per, per)
-        bufs, to = (f_right, to_right) if side == "r" else (f_left, to_left)
+        bufs, to = (f_right if side == "r" else f_left), side_to[side]
         return remote(
             bufs[k - 1].at[part],
             bufs[k].at[part],
@@ -429,12 +432,71 @@
     local.start()
     local.wait()
 
+    def near_copies(coming):
+        out = []
+        for m, off in enumerate((1, -1, 2, -2)):
+            to = (lax.rem(z - off + nz, nz) * NX + x, h)
+            out.append(remote(asks, r["nears"].at[m], r["n_send"].at[m], r["n_recv"].at[m], to))
+        return out
+
+    for copy in near_copies(False):
+        copy.start()
+    nearby = r["nearby"]
+
+    def near_arrive():
+        for copy in near_copies(True):
+            copy.wait_recv()
+        copy = pltpu.make_async_copy(r["nears"], nearby, r["n_local"])
+        copy.start()
+        copy.wait()
+
+    def f_hand(side, g):
+        part = pl.ds(g * few, few)
+        return remote(
+            r["f_pack_" + side].at[part],
+            r["f_next_" + side].at[part],
+            r["fhs_" + side].at[g],
+            r["fhr_" + side].at[g],
+            side_to[side],
+        )
+
+    def f_pass(side):
+        return remote(
+            r["f_next_" + side].at[pl.ds(0, few)],
+            r["f_far_" + side],
+            r["fps_" + side],
+            r["fpr_" + side],
+            side_to[side],
+        )
+
+    def f_pick(side, source):
+        owner = lax.rem(z + nz + (-last if side == "r" else last), nz) * NX + x
+        first, second = ahead[side]
+        pack = r["f_pack_" + side]
+        for i, d in enumerate(far_devices[side]):
+            pack[i] = source[jnp.maximum(nearby[second, d, 0, owner], 0)]
+        for d in range(NX):
+            pack[few + d] = source[jnp.maximum(nearby[first, d, 0, owner], 0)]
+
+    def f_source(zoff, d):
+        if zoff == half:
+            side = "r" if d < few else "l"
+            return r["f_far_" + side].at[d - (0 if d < few else few)]
+        if zoff in (half - 1, half + 1):
+            return r["f_next_" + ("r" if zoff == half + 1 else "l")].at[few + d]
+        return packed.at[d - 1, zoff]
+
+    def f_spread(zoff):
+        for d in range(1, NX):
+            f_copy(zoff, d, False).start()
+        arrived[spot(zoff), 0] = f_source(zoff, 0)[...]
+
     def owner_at(zoff, d):
         return lax.rem(z + zoff, nz) * NX + lax.rem(x + d, NX)
 
     def f_copy(zoff, d, coming):
         return remote(
-            packed.at[d - 1, zoff],
+            f_source(zoff, d),
             arrived.at[spot(zoff), d if coming else NX - d],
             r["fx_send"].at[d - 1, zoff],
             r["fx_recv"].at[d - 1 if coming else NX - d - 1, zoff],
@@ -534,10 +596,15 @@
         feat_t[:, rows] = feat[rows].astype(F32).T.astype(BF16)
 
     def f_done(k):
-        for s in range(SUBS):
-            for side in "rl":
-                if k >= 1 and goes(side, k, s):
+        for side in "rl":
+            if 1 <= k <= last:
+                for s in range(SUBS):
                     f_ring(side, k, s).wait_send()
+            elif k == last + 1:
+                for g in range(3):
+                    f_hand(side, g).wait_send()
+            elif k == half:
+                f_pass(side).wait_send()
         for zoff in offsets(k):
             for d in range(1, NX):
                 f_copy(zoff, d, False).wait_send()
@@ -560,17 +627,41 @@
         if k == 1:
             for copy in hot_copies(True):
                 copy.wait_recv()
-        for s in range(SUBS):
+        if k == last:
+            work = [near_arrive] + work
+        if k <= last:
+            for s in range(SUBS):
+                for side in "rl":
+                    f_ring(side, k, s).wait_recv()
+                    if goes(side, k + 1, s):
+                        f_ring(side, k + 1, s).start()
+                if s < SUBS - 1:
+                    share_out(work, s)
+            if k == last:
+                for side, bufs in (("r", f_right), ("l", f_left)):
+                    f_pick(side, bufs[last])
+                    for g in range(3):
+                        f_hand(side, g).start()
+            f_exchange(nz - k, f_right[k])
+            f_exchange(k, f_left[k])
+            share_out(work, SUBS - 1)
+        elif k == last + 1:
             for side in "rl":
-                if goes(side, k, s):
-                    f_ring(side, k, s).wait_recv()
-                if goes(side, k + 1, s):
-                    f_ring(side, k + 1, s).start()
-            if s == SUBS - 1:
-                f_exchange(nz - k, f_right[k])
-                if k < half:
-                    f_exchange(k, f_left[k])
-            share_out(work, s)
+                f_hand(side, 0).wait_recv()
+                f_pass(side).start()
+            for g in (1, 2):
+                for side in "rl":
+                    f_hand(side, g).wait_recv()
+            f_spread(half + 1)
+            f_spread(half - 1)
+            for item in work:
+                item()
+        else:
+            for side in "rl":
+                f_pass(side).wait_recv()
+            f_spread(half)
+            for item in work:
+                item()
     messages(half)
 
     def finish(j, carry):
@@ -586,9 +677,9 @@
 
     lax.fori_loop(0, blocks, finish, 0)
 
-    back, came, mine, far, near = (r[n] for n in ("back", "came", "mine", "far", "near"))
-    b_right = [r["b_right%d" % k] for k in range(half)]
-    b_left = [r["b_left%d" % k] for k in range(half)]
+    back, came, mine, near = (r[n] for n in ("back", "came", "mine", "near"))
+    b_right = [r["b_right%d" % k] for k in range(last + 1)]
+    b_left = [r["b_left%d" % k] for k in range(last + 1)]
 
     def b_copy(zoff, d, coming):
         return remote(
@@ -614,10 +705,17 @@
         return [functools.partial(b_make, zoff) for zoff in offsets(k)]
 
     def b_done(k):
-        for s in range(SUBS):
-            for side in "rl":
-                if k >= 1 and goes(side, k, s):
+        for side in "rl":
+            if 1 <= k <= last:
+                for s in range(SUBS):
                     b_ring(side, k, s).wait_send()
+            elif k == last + 1:
+                b_onward(side).wait_send()
+                for d in range(NX):
+                    b_hand(side, d).wait_send()
+            elif k == half:
+                for i in range(few):
+                    b_pass(side, i).wait_send()
         for zoff in offsets(k):
             for d in range(1, NX):
                 b_copy(zoff, d, False).wait_send()
@@ -628,15 +726,53 @@
 
     step_rows = min(size, 64)
 
-    def add_local(dst, sources, s, zoff):
-        wanted = [asked[d, 0, owner_at(zoff, 0)] for d in range(NX)]
+    def b_source(zoff, d):
+        return mine.at[zoff] if d == 0 else came.at[d - 1, zoff]
+
+    def b_pass(side, i):
+        return remote(
+            b_source(half, far_devices[side][i]),
+            r["b_far_" + side].at[i],
+            r["bps_" + side].at[i],
+            r["bpr_" + side].at[i],
+            side_to[side],
+        )
+
+    def b_onward(side):
+        return remote(
+            r["b_far_" + side],
+            r["b_next_" + side].at[pl.ds(0, few)],
+            r["bos_" + side],
+            r["bor_" + side],
+            side_to[side],
+        )
+
+    def b_hand(side, d):
+        return remote(
+            b_source(half - 1 if side == "r" else half + 1, d),
+            r["b_next_" + side].at[few + d],
+            r["bhs_" + side].at[d],
+            r["bhr_" + side].at[d],
+            side_to[side],
+        )
+
+    def loose(side):
+        owner = owner_at(last if side == "r" else nz - last, 0)
+        first, second = behind[side]
+        held = r["b_next_" + side]
+        out = [(nearby[second, d, 0, owner], held.at[i]) for i, d in enumerate(far_devices[side])]
+        return out + [(nearby[first, d, 0, owner], held.at[few + d]) for d in range(NX)]
+
+    def add_local(dst, sources, s, zoff, others=()):
+        wanted = [asked[d, 0, owner_at(zoff, 0)] for d in range(NX)] + [place for place, _ in others]
 
         def body(i, carry):
             rows = pl.ds(pl.multiple_of(i * step_rows, step_rows), step_rows)
             terms = [mine[zoff, rows]] + [came[d - 1, zoff, rows] for d in range(1, NX)]
+            terms += [block[rows] for _, block in others]
             for j in range(s * per, (s + 1) * per):
                 sums = None
-                for d in range(NX):
+                for d in range(len(terms)):
                     term = jnp.where(wanted[d] == j, terms[d], jnp.zeros_like(terms[d]))
                     sums = term if sums is None else sums + term
                 for source in sources:
@@ -648,10 +784,9 @@
 
     def b_ring(side, k, s):
         part = pl.ds(s * per, per)
-        bufs, to = (b_right, to_right) if side == "r" else (b_left, to_left)
-        src = far if k == half else bufs[k]
+        bufs, to = (b_right if side == "r" else b_left), side_to[side]
         return remote(
-            src.at[part], bufs[k - 1].at[part], r["bs_" + side].at[k - 1, s], r["br_" + side].at[k - 1, s], to
+            bufs[k].at[part], bufs[k - 1].at[part], r["bs_" + side].at[k - 1, s], r["br_" + side].at[k - 1, s], to
         )
 
     group = selfs.mine.shape[1]
@@ -705,18 +840,40 @@
             work.append(functools.partial(b_done, k + 2))
         for zoff in offsets(k):
             b_arrive(zoff)
-        for s in range(SUBS):
+        if k == half:
+            for i in range(few):
+                for side in "rl":
+                    b_pass(side, i).start()
+            for item in work:
+                item()
+        elif k == last + 1:
+            for d in range(NX):
+                for side in "rl":
+                    b_hand(side, d).start()
             for side in "rl":
-                if not goes(side, k, s):
-                    continue
-                bufs = b_right if side == "r" else b_left
-                sources = []
-                if k < half and goes(side, k + 1, s):
-                    b_ring(side, k + 1, s).wait_recv()
-                    sources = [bufs[k]]
-                add_local(far if k == half else bufs[k], sources, s, k if side == "r" else nz - k)
-                b_ring(side, k, s).start()
-            share_out(work, s)
+                for i in range(few):
+                    b_pass(side, i).wait_recv()
+                b_onward(side).start()
+            for item in work:
+                item()
+        else:
+            if k == last:
+                for side in "rl":
+                    for d in range(NX):
+                        b_hand(side, d).wait_recv()
+                    b_onward(side).wait_recv()
+            for s in range(SUBS):
+                for side in "rl":
+                    bufs = b_right if side == "r" else b_left
+                    sources, others = [], ()
+                    if k < last:
+                        b_ring(side, k + 1, s).wait_recv()
+                        sources = [bufs[k]]
+                    else:
+                        others = loose(side)
+                    add_local(bufs[k], sources, s, k if side == "r" else nz - k, others)
+                    b_ring(side, k, s).start()
+                share_out(work, s)
     b_arrive(0)
     for s in range(SUBS):
         b_ring("r", 1, s).wait_recv()
@@ -726,7 +883,7 @@
     cites.stage1()
     selfs.finish(self_out)
     authors.finish(author_out)
-    for copy in ask_copies(False) + hot_copies(False):
+    for copy in ask_copies(False) + hot_copies(False) + near_copies(False):
         copy.wait_send()
     for k in (2, 1, 0):
         b_done(k)
@@ -772,7 +929,6 @@
         "back": column,
         "came": column,
         "mine": pltpu.VMEM((nz, size, width), BF16),
-        "far": chunk,
         "near": chunk,
         "h_send": dma((nh - 1,)),
         "h_recv": dma((nh - 1,)),
@@ -780,15 +936,30 @@
         "q_recv": dma((NX - 1,)),
         "q_local": dma,
     }
-    for k in range(1, half + 1):
-        scratch["f_right%d" % k] = chunk
-    for k in range(1, half):
-        scratch["f_left%d" % k] = chunk
-    for k in range(half):
-        scratch["b_right%d" % k] = chunk
-        scratch["b_left%d" % k] = chunk
+    few = NX // 2
+    several = pltpu.VMEM((NX + few, size, width), BF16)
+    scratch["nears"] = pltpu.VMEM((4, NX) + req.shape, jnp.int32)
+    scratch["nearby"] = pltpu.SMEM((4, NX) + req.shape, jnp.int32)
+    scratch["n_send"] = dma((4,))
+    scratch["n_recv"] = dma((4,))
+    scratch["n_local"] = dma
+    for side, word in (("r", "right"), ("l", "left")):
+        for k in range(1, half - 1):
+            scratch["f_%s%d" % (word, k)] = chunk
+        for k in range(half - 1):
+            scratch["b_%s%d" % (word, k)] = chunk
+        for name in ("f_pack_", "f_next_", "b_next_"):
+            scratch[name + side] = several
+        for name in ("f_far_", "b_far_"):
+            scratch[name + side] = pltpu.VMEM((few, size, width), BF16)
+        for name, count in (("fh", 3), ("bp", few), ("bh", NX)):
+            scratch[name + "s_" + side] = dma((count,))
+            scratch[name + "r_" + side] = dma((count,))
+        for name in ("fp", "bo"):
+            scratch[name + "s_" + side] = dma
+            scratch[name + "r_" + side] = dma
     for name in ("fs_r", "fr_r", "fs_l", "fr_l", "bs_r", "br_r", "bs_l", "br_l"):
-        scratch[name] = dma((half, SUBS))
+        scratch[name] = dma((half - 2, SUBS))
     for name in ("fx_send", "fx_recv", "bx_send", "bx_recv"):
         scratch[name] = dma((NX - 1, nz))
     for name, parts in (

time: 238 us -> 230 us (0.966)
  Pallas kernels: 235 us -> 228 us
    pallas_call x1, Pallas kernels: 234 us -> 226 us  [layer(): pl.pallas_call(functools.partial(layer_kernel, names, nz, nh), out_shape=...]
where the time goes in v5:
time: 230 us
  Pallas kernels  228 us (99%)
    pallas_call x1, Pallas kernels, layer(): pl.pallas_call(functools.partial(layer_kernel, names, nz, nh), out_shape=...  226 us

profile of v5, /device:TPU:17, one launch (start us, length us, event | category | flops | bytes accessed | tf_op | source)
XLA Modules:
  0.0 229.9 jit_solution(10267649751900933928)
XLA Ops:
  0.6 1.4 select_reduce_fusion.refs_5_
  2.0 225.9 %shard_map.138 = (bf16[1024,256]{1,0:T(8,128)(2,1)}, f32[12,256]{1,0:T(8,128)}, f32[12,256]{1,0:T(8,128)}, f32[128,256]{1,0:T(8,128)}) custom-call(bf16[1024,768]{1,0:T(8,128)(2,1)} %refs_0_.1, bf16[768,256]{1,0:T(8,128)(2,1)} %refs_1_.1, bf16[768,256]{1,0:T(8,128)(2,1)} %refs_2_.1, f32[128,256]{1,0:T(8,128)} %refs_3_.1, s32[8,1024]{1,0:T(8,128)} %bitcast.1, ...), custom_call_target="tpu_custom_call" | custom-call | tf_op jit(solution)/shard_map/pallas_call | solution.py:973
  227.9 2.0 shard_map.139
  (1 shorter events, 0.0 us)

commit v6 on v5

--- a/solution.py
+++ b/solution.py
@@ -376,6 +376,10 @@
     ahead = {"r": (0, 2), "l": (1, 3)}
     behind = {"r": (1, 3), "l": (0, 2)}
     side_to = {"r": to_right, "l": to_left}
+    side_two = {
+        "r": (lax.rem(z + 2, nz) * NX + x, h),
+        "l": (lax.rem(z + nz - 2, nz) * NX + x, h),
+    }
 
     def goes(side, k, s):
         return k <= last
@@ -392,11 +396,14 @@
         )
 
     def project(j, carry):
-        rows = pl.ds(pl.multiple_of(j * size, size), size)
-        own[j] = jnp.dot(feat[rows], w_cite[...], preferred_element_type=F32).astype(BF16)
+        many = blocks // 2
+        rows = pl.ds(pl.multiple_of(j * many * size, many * size), many * size)
+        value = jnp.dot(feat[rows], w_cite[...], preferred_element_type=F32).astype(BF16)
+        for i in range(many):
+            own[j * many + i] = value[i * size : (i + 1) * size]
         return carry
 
-    lax.fori_loop(0, blocks, project, 0)
+    lax.fori_loop(0, 2, project, 0)
     wait_all()
     for s in range(SUBS):
         for side in "rl":
@@ -452,20 +459,19 @@
 
     def f_hand(side, g):
         part = pl.ds(g * few, few)
+        if g == 0:
+            return remote(
+                r["f_pack_" + side].at[part],
+                r["f_far_" + side],
+                r["fps_" + side],
+                r["fpr_" + side],
+                side_two[side],
+            )
         return remote(
             r["f_pack_" + side].at[part],
             r["f_next_" + side].at[part],
             r["fhs_" + side].at[g],
             r["fhr_" + side].at[g],
-            side_to[side],
-        )
-
-    def f_pass(side):
-        return remote(
-            r["f_next_" + side].at[pl.ds(0, few)],
-            r["f_far_" + side],
-            r["fps_" + side],
-            r["fpr_" + side],
             side_to[side],
         )
 
@@ -603,8 +609,6 @@
             elif k == last + 1:
                 for g in range(3):
                     f_hand(side, g).wait_send()
-            elif k == half:
-                f_pass(side).wait_send()
         for zoff in offsets(k):
             for d in range(1, NX):
                 f_copy(zoff, d, False).wait_send()
@@ -646,9 +650,6 @@
             f_exchange(k, f_left[k])
             share_out(work, SUBS - 1)
         elif k == last + 1:
-            for side in "rl":
-                f_hand(side, 0).wait_recv()
-                f_pass(side).start()
             for g in (1, 2):
                 for side in "rl":
                     f_hand(side, g).wait_recv()
@@ -658,7 +659,7 @@
                 item()
         else:
             for side in "rl":
-                f_pass(side).wait_recv()
+                f_hand(side, 0).wait_recv()
             f_spread(half)
             for item in work:
                 item()
@@ -710,7 +711,6 @@
                 for s in range(SUBS):
                     b_ring(side, k, s).wait_send()
             elif k == last + 1:
-                b_onward(side).wait_send()
                 for d in range(NX):
                     b_hand(side, d).wait_send()
             elif k == half:
@@ -732,19 +732,10 @@
     def b_pass(side, i):
         return remote(
             b_source(half, far_devices[side][i]),
-            r["b_far_" + side].at[i],
+            r["b_next_" + side].at[i],
             r["bps_" + side].at[i],
             r["bpr_" + side].at[i],
-            side_to[side],
-        )
-
-    def b_onward(side):
-        return remote(
-            r["b_far_" + side],
-            r["b_next_" + side].at[pl.ds(0, few)],
-            r["bos_" + side],
-            r["bor_" + side],
-            side_to[side],
+            side_two[side],
         )
 
     def b_hand(side, d):
@@ -850,10 +841,6 @@
             for d in range(NX):
                 for side in "rl":
                     b_hand(side, d).start()
-            for side in "rl":
-                for i in range(few):
-                    b_pass(side, i).wait_recv()
-                b_onward(side).start()
             for item in work:
                 item()
         else:
@@ -861,7 +848,8 @@
                 for side in "rl":
                     for d in range(NX):
                         b_hand(side, d).wait_recv()
-                    b_onward(side).wait_recv()
+                    for i in range(few):
+                        b_pass(side, i).wait_recv()
             for s in range(SUBS):
                 for side in "rl":
                     bufs = b_right if side == "r" else b_left
@@ -950,14 +938,12 @@
             scratch["b_%s%d" % (word, k)] = chunk
         for name in ("f_pack_", "f_next_", "b_next_"):
             scratch[name + side] = several
-        for name in ("f_far_", "b_far_"):
-            scratch[name + side] = pltpu.VMEM((few, size, width), BF16)
+        scratch["f_far_" + side] = pltpu.VMEM((few, size, width), BF16)
         for name, count in (("fh", 3), ("bp", few), ("bh", NX)):
             scratch[name + "s_" + side] = dma((count,))
             scratch[name + "r_" + side] = dma((count,))
-        for name in ("fp", "bo"):
-            scratch[name + "s_" + side] = dma
-            scratch[name + "r_" + side] = dma
+        scratch["fps_" + side] = dma
+        scratch["fpr_" + side] = dma
     for name in ("fs_r", "fr_r", "fs_l", "fr_l", "bs_r", "br_r", "bs_l", "br_l"):
         scratch[name] = dma((half - 2, SUBS))
     for name in ("fx_send", "fx_recv", "bx_send", "bx_recv"):

time: 230 us -> 234 us (1.017)
  Pallas kernels: 228 us -> 231 us
    pallas_call x1, Pallas kernels: 226 us -> 229 us  [layer(): pl.pallas_call(functools.partial(layer_kernel, names, nz, nh), out_shape=...]
where the time goes in v6:
time: 234 us; the launch traced here: 233 us
  Pallas kernels  231 us (99%)
    pallas_call x1, Pallas kernels, layer(): pl.pallas_call(functools.partial(layer_kernel, names, nz, nh), out_shape=...  229 us

profile of v6, /device:TPU:17, one launch (start us, length us, event | category | flops | bytes accessed | tf_op | source)
XLA Modules:
  0.0 233.4 jit_solution(804598717393232815)
XLA Ops:
  0.6 1.4 select_reduce_fusion.refs_5_
  2.0 229.4 %shard_map.138 = (bf16[1024,256]{1,0:T(8,128)(2,1)}, f32[12,256]{1,0:T(8,128)}, f32[12,256]{1,0:T(8,128)}, f32[128,256]{1,0:T(8,128)}) custom-call(bf16[1024,768]{1,0:T(8,128)(2,1)} %refs_0_.1, bf16[768,256]{1,0:T(8,128)(2,1)} %refs_1_.1, bf16[768,256]{1,0:T(8,128)(2,1)} %refs_2_.1, f32[128,256]{1,0:T(8,128)} %refs_3_.1, s32[8,1024]{1,0:T(8,128)} %bitcast.1, ...), custom_call_target="tpu_custom_call" | custom-call | tf_op jit(solution)/shard_map/pallas_call | solution.py:959
  231.4 2.0 shard_map.139
  (1 shorter events, 0.0 us)

commit v7 on v5

--- a/solution.py
+++ b/solution.py
@@ -392,11 +392,14 @@
         )
 
     def project(j, carry):
-        rows = pl.ds(pl.multiple_of(j * size, size), size)
-        own[j] = jnp.dot(feat[rows], w_cite[...], preferred_element_type=F32).astype(BF16)
+        many = blocks // 2
+        rows = pl.ds(pl.multiple_of(j * many * size, many * size), many * size)
+        value = jnp.dot(feat[rows], w_cite[...], preferred_element_type=F32).astype(BF16)
+        for i in range(many):
+            own[j * many + i] = value[i * size : (i + 1) * size]
         return carry
 
-    lax.fori_loop(0, blocks, project, 0)
+    lax.fori_loop(0, 2, project, 0)
     wait_all()
     for s in range(SUBS):
         for side in "rl":

time: 230 us -> 230 us (level)
  no operation moved by 1% of the time
where the time goes in v7:
time: 230 us
  Pallas kernels  228 us (99%)
    pallas_call x1, Pallas kernels, layer(): pl.pallas_call(functools.partial(layer_kernel, names, nz, nh), out_shape=...  226 us

profile of v7, /device:TPU:17, one launch (start us, length us, event | category | flops | bytes accessed | tf_op | source)
XLA Modules:
  0.0 230.1 jit_solution(5120853771952110375)
XLA Ops:
  0.6 1.4 select_reduce_fusion.refs_5_
  2.0 226.1 %shard_map.138 = (bf16[1024,256]{1,0:T(8,128)(2,1)}, f32[12,256]{1,0:T(8,128)}, f32[12,256]{1,0:T(8,128)}, f32[128,256]{1,0:T(8,128)}) custom-call(bf16[1024,768]{1,0:T(8,128)(2,1)} %refs_0_.1, bf16[768,256]{1,0:T(8,128)(2,1)} %refs_1_.1, bf16[768,256]{1,0:T(8,128)(2,1)} %refs_2_.1, f32[128,256]{1,0:T(8,128)} %refs_3_.1, s32[8,1024]{1,0:T(8,128)} %bitcast.1, ...), custom_call_target="tpu_custom_call" | custom-call | tf_op jit(solution)/shard_map/pallas_call | solution.py:976
  228.2 2.0 shard_map.139
  (1 shorter events, 0.0 us)
